TPU v7x, 32 devices: a whole 2x2x4 slice. The times are simulated.
32 devices in a mesh: section: 2 (over core), dp: 4 (over z), tensor: 4 (over y, x).
Axes of the slice: x: 2, y: 2, z: 4, core: 2. Of those that a mesh axis runs over, the one named last changes fastest.
Arguments:
- inputs: bfloat16 [2, 4096, 768], P(None, ('dp', 'tensor')), may hold values from -6 to 6
- cotangent: bfloat16 [2, 4096, 768], P(None, ('dp', 'tensor')), may hold values from -6 to 6
- seq_lengths: int32 [2, 4, 8], P(None, 'dp'), may hold values from 0 to 1024, as said below
- norm_gain: float32 [2, 2, 768], P('section'), may hold values from 0.25 to 1.75
- norm_shift: float32 [2, 2, 768], P('section'), may hold values from -1 to 1
- w_qkv: bfloat16 [2, 3, 768, 768], P('section', None, 'dp', 'tensor'), may hold values from -0.21875 to 0.21875
- b_qv: float32 [2, 2, 768], P('section', None, 'tensor'), may hold values from -1.5 to 1.5
- w_out: bfloat16 [2, 768, 768], P('section', 'tensor', 'dp'), may hold values from -0.875 to 0.875
- b_out: float32 [2, 768], P('section'), may hold values from -1 to 1
- w_up: bfloat16 [2, 768, 3072], P('section', 'dp', 'tensor'), may hold values from -0.21875 to 0.21875
- b_up: float32 [2, 3072], P('section', 'tensor'), may hold values from -1.5 to 1.5
- w_down: bfloat16 [2, 3072, 768], P('section', 'tensor', 'dp'), may hold values from -0.15625 to 0.15625
- b_down: float32 [2, 768], P('section'), may hold values from -1 to 1
Outputs:
- layer_out: bfloat16 [2, 2, 4096, 768], P('section', None, ('dp', 'tensor'))
- input_grad: bfloat16 [2, 2, 4096, 768], P('section', None, ('dp', 'tensor'))
- grad_norm_gain: float32 [2, 2, 768], P('section')
- grad_norm_shift: float32 [2, 2, 768], P('section')
- grad_w_qkv: float32 [2, 3, 768, 768], P('section', None, 'dp', 'tensor')
- grad_b_qv: float32 [2, 2, 768], P('section', None, 'tensor')
- grad_w_out: float32 [2, 768, 768], P('section', 'tensor', 'dp')
- grad_b_out: float32 [2, 768], P('section')
- grad_w_up: float32 [2, 768, 3072], P('section', 'dp', 'tensor')
- grad_b_up: float32 [2, 3072], P('section', 'tensor')
- grad_w_down: float32 [2, 3072, 768], P('section', 'tensor', 'dp')
- grad_b_down: float32 [2, 768], P('section')
Inputs may be any that keep to these rules, and one draw needn't show every extreme that they name: `seq_lengths`: in each micro-batch and data shard the sequences fill the slots from the first; a slot of length 0 holds no sequence; the lengths of one micro-batch on one data shard add up to at most 1024, exactly 1024 on some shard, and some sequence has length 1024.
All inputs are finite; a program needn't handle non-finite values.
Results may differ from a plain program's by a relative error of at most 0.02.
Values may be sent and summed in bfloat16 or wider, within the bound.
No kernel may reach another device: no remote copies, remote signals or barrier semaphores. Data moves between devices by JAX's collectives and lax.ppermute only.
A program may use at most 192 MiB of HBM per device.

v0:
```python
import jax
import jax.numpy as jnp
from jax import lax
from jax.sharding import PartitionSpec as P

HD = 64


def passed_along(shard, axis, by):
    count = lax.axis_size(axis)
    pairs = [(i, i + by) for i in range(count) if 0 <= i + by < count]
    return lax.ppermute(shard, axis, pairs)


def norm_rows(values, norm_scale, norm_bias):
    row_mean = jnp.mean(values, axis=-1, keepdims=True)
    centred = values - row_mean
    row_var = jnp.mean(centred * centred, axis=-1, keepdims=True)
    return centred * lax.rsqrt(row_var + 1e-05) * norm_scale + norm_bias


def smooth_gate(values):
    return jax.nn.gelu(values, approximate=False)


def segments_of(lengths, total_rows):
    seq_ends = jnp.cumsum(lengths)
    places = jnp.arange(total_rows, dtype=jnp.int32)
    labels = jnp.sum((places[:, None] >= seq_ends[None, :]).astype(jnp.int32), axis=1)
    inside = places < seq_ends[-1]
    return (jnp.where(inside, labels, lengths.shape[0] + places), inside)


def block_scores(query_block, keys, labels, row_start, block_rows):
    scores = jnp.einsum("qhd,khd->hqk", query_block, keys, preferred_element_type=jnp.float32)
    places = jnp.arange(keys.shape[0], dtype=jnp.int32)
    own_rows = row_start + jnp.arange(block_rows, dtype=jnp.int32)
    own_labels = lax.dynamic_slice_in_dim(labels, row_start, block_rows)
    allowed = (own_labels[:, None] == labels[None, :]) & (own_rows[:, None] >= places[None, :])
    return jnp.where(allowed[None], scores, -1000000000.0)


def attend_forward(query, keys, values, labels):
    total_rows = query.shape[0]
    block_rows = min(512, total_rows)

    def one_block(block_index):
        row_start = block_index * block_rows
        query_block = lax.dynamic_slice_in_dim(query, row_start, block_rows, 0)
        scores = block_scores(query_block, keys, labels, row_start, block_rows)
        row_max = jnp.max(scores, axis=-1, keepdims=True)
        weights = jnp.exp(scores - row_max)
        row_total = jnp.sum(weights, axis=-1, keepdims=True)
        probs = (weights / row_total).astype(jnp.bfloat16)
        mixed = jnp.einsum("hqk,khd->qhd", probs, values, preferred_element_type=jnp.float32)
        return (mixed.astype(jnp.bfloat16), row_max, row_total)

    mixed, row_max, row_total = lax.map(
        one_block, jnp.arange(total_rows // block_rows, dtype=jnp.int32)
    )
    return (mixed.reshape(query.shape), row_max, row_total)


def attend_backward(query, keys, values, labels, row_max, row_total, grad_mixed):
    total_rows = query.shape[0]
    block_rows = min(512, total_rows)

    def one_block(carry, block_index):
        grad_keys, grad_values = carry
        row_start = block_index * block_rows
        query_block = lax.dynamic_slice_in_dim(query, row_start, block_rows, 0)
        grad_block = lax.dynamic_slice_in_dim(grad_mixed, row_start, block_rows, 0)
        scores = block_scores(query_block, keys, labels, row_start, block_rows)
        probs = jnp.exp(scores - row_max[block_index]) / row_total[block_index]
        grad_values = grad_values + jnp.einsum(
            "hqk,qhd->khd",
            probs.astype(jnp.bfloat16),
            grad_block,
            preferred_element_type=jnp.float32,
        )
        grad_probs = jnp.einsum(
            "qhd,khd->hqk", grad_block, values, preferred_element_type=jnp.float32
        )
        inner = jnp.sum(grad_probs * probs, axis=-1, keepdims=True)
        grad_scores = (probs * (grad_probs - inner)).astype(jnp.bfloat16)
        grad_query = jnp.einsum(
            "hqk,khd->qhd", grad_scores, keys, preferred_element_type=jnp.float32
        )
        grad_keys = grad_keys + jnp.einsum(
            "hqk,qhd->khd", grad_scores, query_block, preferred_element_type=jnp.float32
        )
        return ((grad_keys, grad_values), grad_query)

    zero_keys = jnp.zeros(keys.shape, jnp.float32)
    (grad_keys, grad_values), grad_query = lax.scan(
        one_block, (zero_keys, zero_keys), jnp.arange(total_rows // block_rows, dtype=jnp.int32)
    )
    return (grad_query.reshape(query.shape), grad_keys, grad_values)


def layer_forward(state, params, labels):
    (
        gains,
        shifts,
        qkv_cat,
        q_bias,
        v_bias,
        out_weight,
        out_bias,
        up_weight,
        up_bias,
        down_weight,
        down_bias,
    ) = params
    head_width = q_bias.shape[0]
    scale = HD ** (-0.5)
    normed = norm_rows(state, gains[0], shifts[0]).astype(jnp.bfloat16)
    gathered = lax.all_gather(normed, "tensor", axis=0, tiled=True)
    total_rows = gathered.shape[0]
    projected = jnp.dot(gathered, qkv_cat, preferred_element_type=jnp.float32)
    query = ((projected[:, :head_width] + q_bias) * scale).astype(jnp.bfloat16)
    keys = projected[:, head_width : 2 * head_width].astype(jnp.bfloat16)
    values = (projected[:, 2 * head_width :] + v_bias).astype(jnp.bfloat16)
    heads_here = head_width // HD
    query = query.reshape(total_rows, heads_here, HD)
    keys = keys.reshape(total_rows, heads_here, HD)
    values = values.reshape(total_rows, heads_here, HD)
    mixed, row_max, row_total = attend_forward(query, keys, values, labels)
    mixed = mixed.reshape(total_rows, head_width)
    rows_here = mixed
    middle = (
        state
        + lax.psum_scatter(
            jnp.dot(rows_here, out_weight, preferred_element_type=jnp.float32).astype(jnp.bfloat16),
            "tensor",
            scatter_dimension=0,
            tiled=True,
        ).astype(jnp.float32)
        + out_bias
    )
    normed_mid = norm_rows(middle, gains[1], shifts[1]).astype(jnp.bfloat16)
    gathered_mid = lax.all_gather(normed_mid, "tensor", axis=0, tiled=True)
    hidden_pre = jnp.dot(gathered_mid, up_weight, preferred_element_type=jnp.float32) + up_bias
    hidden = smooth_gate(hidden_pre).astype(jnp.bfloat16)
    rows_here = hidden
    result = (
        middle
        + lax.psum_scatter(
            jnp.dot(rows_here, down_weight, preferred_element_type=jnp.float32).astype(
                jnp.bfloat16
            ),
            "tensor",
            scatter_dimension=0,
            tiled=True,
        ).astype(jnp.float32)
        + down_bias
    )
    kept = (
        state,
        gathered,
        query,
        keys,
        values,
        row_max,
        row_total,
        mixed,
        middle,
        gathered_mid,
        hidden_pre,
        hidden,
    )
    return (result, kept)


def layer_backward(grad_out, params, kept, labels):
    (
        gains,
        shifts,
        qkv_cat,
        q_bias,
        v_bias,
        out_weight,
        out_bias,
        up_weight,
        up_bias,
        down_weight,
        down_bias,
    ) = params
    (
        state,
        gathered,
        query,
        keys,
        values,
        row_max,
        row_total,
        mixed,
        middle,
        gathered_mid,
        hidden_pre,
        hidden,
    ) = kept
    head_width = q_bias.shape[0]
    total_rows = gathered.shape[0]
    scale = HD ** (-0.5)
    grad_down_bias = jnp.sum(grad_out, axis=0)
    grad_full = lax.all_gather(grad_out.astype(jnp.bfloat16), "tensor", axis=0, tiled=True)
    grad_down_w = jnp.einsum("rf,rd->fd", hidden, grad_full, preferred_element_type=jnp.float32)
    grad_hidden = jnp.einsum(
        "rd,fd->rf", grad_full, down_weight, preferred_element_type=jnp.float32
    )
    _, gate_back = jax.vjp(smooth_gate, hidden_pre)
    grad_pre = gate_back(grad_hidden)[0].astype(jnp.bfloat16)
    grad_up_bias = jnp.sum(grad_pre.astype(jnp.float32), axis=0)
    grad_up_w = jnp.einsum("rd,rf->df", gathered_mid, grad_pre, preferred_element_type=jnp.float32)
    rows_here = grad_pre
    grad_normed_mid = lax.psum_scatter(
        jnp.einsum("rf,df->rd", rows_here, up_weight, preferred_element_type=jnp.float32).astype(
            jnp.bfloat16
        ),
        "tensor",
        scatter_dimension=0,
        tiled=True,
    ).astype(jnp.float32)
    _, norm_back_mid = jax.vjp(norm_rows, middle, gains[1], shifts[1])
    grad_mid_norm, grad_gain_mid, grad_shift_mid = norm_back_mid(grad_normed_mid)
    grad_middle = grad_out + grad_mid_norm
    grad_out_bias = jnp.sum(grad_middle, axis=0)
    grad_mid_full = lax.all_gather(grad_middle.astype(jnp.bfloat16), "tensor", axis=0, tiled=True)
    grad_out_w = jnp.einsum("re,rd->ed", mixed, grad_mid_full, preferred_element_type=jnp.float32)
    grad_mixed = jnp.einsum(
        "rd,ed->re", grad_mid_full, out_weight, preferred_element_type=jnp.float32
    ).astype(jnp.bfloat16)
    heads_here = head_width // HD
    grad_query, grad_keys, grad_values = attend_backward(
        query,
        keys,
        values,
        labels,
        row_max,
        row_total,
        grad_mixed.reshape(total_rows, heads_here, HD),
    )
    grad_query = (grad_query.astype(jnp.bfloat16).astype(jnp.float32) * scale).astype(jnp.bfloat16)
    grad_query = grad_query.reshape(total_rows, head_width)
    grad_keys = grad_keys.astype(jnp.bfloat16).reshape(total_rows, head_width)
    grad_values = grad_values.astype(jnp.bfloat16).reshape(total_rows, head_width)
    grad_q_bias = jnp.sum(grad_query.astype(jnp.float32), axis=0)
    grad_v_bias = jnp.sum(grad_values.astype(jnp.float32), axis=0)
    grad_proj = jnp.concatenate([grad_query, grad_keys, grad_values], axis=1)
    grad_qkv_w = jnp.einsum("rd,re->de", gathered, grad_proj, preferred_element_type=jnp.float32)
    rows_here = grad_proj
    grad_normed = lax.psum_scatter(
        jnp.einsum("re,de->rd", rows_here, qkv_cat, preferred_element_type=jnp.float32).astype(
            jnp.bfloat16
        ),
        "tensor",
        scatter_dimension=0,
        tiled=True,
    ).astype(jnp.float32)
    _, norm_back = jax.vjp(norm_rows, state, gains[0], shifts[0])
    grad_state_norm, grad_gain_first, grad_shift_first = norm_back(grad_normed)
    grad_state = grad_middle + grad_state_norm
    model_width = gathered.shape[1]
    grad_qkv_three = jnp.transpose(grad_qkv_w.reshape(model_width, 3, head_width), (1, 0, 2))
    matrices = (grad_qkv_three, grad_out_w, grad_up_w, grad_down_w)
    smalls = (
        jnp.stack([grad_gain_first, grad_gain_mid]),
        jnp.stack([grad_shift_first, grad_shift_mid]),
        jnp.stack([grad_q_bias, grad_v_bias]),
        grad_out_bias,
        grad_up_bias,
        grad_down_bias,
    )
    return (grad_state, matrices, smalls)


def add_trees(first_tree, second_tree):
    return jax.tree.map(jnp.add, first_tree, second_tree)


def stack_all(*members):
    return jnp.stack(members)


def shards(
    inputs,
    cotangent,
    seq_lengths,
    norm_gain,
    norm_shift,
    w_qkv,
    b_qv,
    w_out,
    b_out,
    w_up,
    b_up,
    w_down,
    b_down,
):
    section_rank = lax.axis_index("section")
    tensor_rank = lax.axis_index("tensor")
    is_first = section_rank == 0
    micro = inputs.shape[0]
    local_rows = inputs.shape[1]
    total_rows = local_rows * lax.axis_size("tensor")
    first_row = tensor_rank * local_rows
    full_qkv, full_out, full_up, full_down = (
        lax.all_gather(w_qkv, "dp", axis=2, tiled=True),
        lax.all_gather(w_out, "dp", axis=2, tiled=True),
        lax.all_gather(w_up, "dp", axis=1, tiled=True),
        lax.all_gather(w_down, "dp", axis=2, tiled=True),
    )
    head_width = full_qkv.shape[3]
    model_width = full_qkv.shape[2]
    hidden_width = full_up.shape[2]
    qkv_cat = jnp.transpose(full_qkv[0], (1, 0, 2)).reshape(model_width, 3 * head_width)
    params = (
        norm_gain[0],
        norm_shift[0],
        qkv_cat,
        b_qv[0, 0],
        b_qv[0, 1],
        full_out[0],
        b_out[0],
        full_up[0],
        b_up[0],
        full_down[0],
        b_down[0],
    )
    lengths_all = seq_lengths[:, 0, :]
    ticks = micro + 1
    arrived = jnp.zeros((local_rows, model_width), jnp.bfloat16)
    forward_outs = []
    saved = []
    for tick_index in range(ticks):
        own_micro = jnp.clip(tick_index - section_rank, 0, micro - 1)
        lengths = lax.dynamic_index_in_dim(lengths_all, own_micro, 0, keepdims=False)
        labels, inside = segments_of(lengths, total_rows)
        inside_local = lax.dynamic_slice_in_dim(inside, first_row, local_rows)
        start_state = jnp.where(is_first, inputs[min(tick_index, micro - 1)], arrived).astype(
            jnp.float32
        )
        result, kept = layer_forward(start_state, params, labels)
        rounded = result.astype(jnp.bfloat16)
        forward_outs.append(rounded)
        saved.append(kept + (labels, inside_local))
        if tick_index + 1 < ticks:
            arrived = passed_along(rounded, "section", 1)
    layer_out = lax.dynamic_slice_in_dim(jnp.stack(forward_outs), section_rank, micro, 0)[None]
    store = jax.tree.map(stack_all, *saved)
    returned = jnp.zeros((local_rows, model_width), jnp.bfloat16)
    backward_outs = []
    matrix_total = None
    small_total = None
    for tick_index in range(ticks):
        saved_index = jnp.clip(tick_index - 1 + 2 * section_rank, 0, micro)
        kept = jax.tree.map(
            lambda member: lax.dynamic_index_in_dim(member, saved_index, 0, keepdims=False), store
        )
        labels = kept[-2]
        inside_local = kept[-1]
        live = jnp.where(is_first, tick_index >= 1, tick_index < micro).astype(jnp.float32)
        from_cot = cotangent[min(tick_index, micro - 1)].astype(jnp.float32) * inside_local[
            :, None
        ].astype(jnp.float32)
        incoming = jnp.where(is_first, returned.astype(jnp.float32), from_cot) * live
        grad_state, matrices, smalls = layer_backward(incoming, params, kept[:-2], labels)
        rounded = grad_state.astype(jnp.bfloat16)
        backward_outs.append(rounded)
        if tick_index + 1 < ticks:
            returned = passed_along(rounded, "section", -1)
        matrices = (
            lax.psum_scatter(
                matrices[0].astype(jnp.bfloat16), "dp", scatter_dimension=1, tiled=True
            ).astype(jnp.float32),
            lax.psum_scatter(
                matrices[1].astype(jnp.bfloat16), "dp", scatter_dimension=1, tiled=True
            ).astype(jnp.float32),
            lax.psum_scatter(
                matrices[2].astype(jnp.bfloat16), "dp", scatter_dimension=0, tiled=True
            ).astype(jnp.float32),
            lax.psum_scatter(
                matrices[3].astype(jnp.bfloat16), "dp", scatter_dimension=1, tiled=True
            ).astype(jnp.float32),
        )
        matrix_total = matrices if matrix_total is None else add_trees(matrix_total, matrices)
        small_total = smalls if small_total is None else add_trees(small_total, smalls)
    input_grad = lax.dynamic_slice_in_dim(jnp.stack(backward_outs), 1 - section_rank, micro, 0)[
        None
    ]
    grad_qkv_w, grad_out_w, grad_up_w, grad_down_w = matrix_total
    gain_grad, shift_grad, qv_grad, out_bias_grad, up_bias_grad, down_bias_grad = small_total
    column_start = tensor_rank * head_width
    qv_wide = lax.dynamic_update_slice(
        jnp.zeros((2, model_width), jnp.float32), qv_grad, (jnp.int32(0), column_start)
    )
    up_start = tensor_rank * hidden_width
    up_wide = lax.dynamic_update_slice(
        jnp.zeros((hidden_width * lax.axis_size("tensor"),), jnp.float32), up_bias_grad, (up_start,)
    )
    gain_sum, shift_sum, out_bias_sum, down_bias_sum, qv_sum, up_sum = lax.psum(
        (gain_grad, shift_grad, out_bias_grad, down_bias_grad, qv_wide, up_wide), ("dp", "tensor")
    )
    qv_own = lax.dynamic_slice_in_dim(qv_sum, column_start, head_width, 1)
    up_own = lax.dynamic_slice_in_dim(up_sum, up_start, hidden_width, 0)
    return (
        layer_out,
        input_grad,
        gain_sum[None],
        shift_sum[None],
        grad_qkv_w[None],
        qv_own[None],
        grad_out_w[None],
        out_bias_sum[None],
        grad_up_w[None],
        up_own[None],
        grad_down_w[None],
        down_bias_sum[None],
    )


def solution(mesh):
    in_specs = (
        P(None, ("dp", "tensor"), None),
        P(None, ("dp", "tensor"), None),
        P(None, "dp", None),
        P("section", None, None),
        P("section", None, None),
        P("section", None, "dp", "tensor"),
        P("section", None, "tensor"),
        P("section", "tensor", "dp"),
        P("section", None),
        P("section", "dp", "tensor"),
        P("section", "tensor"),
        P("section", "tensor", "dp"),
        P("section", None),
    )
    out_specs = (
        P("section", None, ("dp", "tensor"), None),
        P("section", None, ("dp", "tensor"), None),
        P("section", None, None),
        P("section", None, None),
        P("section", None, "dp", "tensor"),
        P("section", None, "tensor"),
        P("section", "tensor", "dp"),
        P("section", None),
        P("section", "dp", "tensor"),
        P("section", "tensor"),
        P("section", "tensor", "dp"),
        P("section", None),
    )
    return jax.shard_map(shards, mesh=mesh, in_specs=in_specs, out_specs=out_specs, check_vma=False)
```

profile of v0, /device:TPU:0, one launch (start us, length us, event | category | flops | bytes accessed | tf_op | source)
XLA Modules:
  0.0 1526.5 jit_solution(13331410886029463100)
XLA Ops:
  18.4 21.3 %all_gather.50 = bf16[1,192,768]{1,0,2:T(2,128)(2,1)S(1)} all-gather(bf16[1,192,192]{1,0,2:T(2,128)(2,1)S(1)} %copy.67), channel_id=1, replica_groups=mesh['section'=2,'dp'=4,'tensor'=4] {'dp'}, dimensions={2}, use_global_device_ids=true | all-gather | bytes 368640 | tf_op jit(solution)/shard_map/all_gather | solution.py:310
  40.2 27.1 %all_gather.49 = bf16[1,3,768,192]{3,1,0,2:T(4,128)(2,1)S(1)} all-gather(bf16[1,3,192,192]{3,1,0,2:T(4,128)(2,1)S(1)} %copy.64), channel_id=1, replica_groups=mesh['section'=2,'dp'=4,'tensor'=4] {'dp'}, dimensions={2}, use_global_device_ids=true | all-gather | bytes 1105920 | tf_op jit(solution)/shard_map/all_gather | solution.py:309
  72.7 17.8 %while.87 = (s32[]{:T(128)}, bf16[2,512,3,64]{1,3,2,0:T(8,128)(2,1)S(1)}, f32[2,3,512,1]{2,1,3,0:T(4,128)S(1)}, f32[2,3,512,1]{2,1,3,0:T(4,128)S(1)}, s32[2]{0:T...) while((s32[]{:T(128)}, ...), condition=%wide.region_7.8_spmd, body=%wide.region_4.7_spmd.sunk | while | flops 418477568 | bytes 22233300 | solution.py:58
  93.6 31.5 %reduce-scatter.37.cloned.1.call-done = bf16[256,768]{1,0:T(8,128)(2,1)} async-done(((bf16[1024,768]{1,0:T(8,128)(2,1)}), bf16[256,768]{1,0:T(8,128)(2,1)}) %reduce-scatter.37.cloned.1.call-update) | async-done | bytes 393232 | tf_op jit(solution)/shard_map/reduce_scatter | solution.py:133
  131.4 30.1 %all-gather.17.cloned.1.call-done = bf16[1024,768]{1,0:T(8,128)(2,1)} async-done(((bf16[256,768]{1,0:T(8,128)(2,1)}), bf16[1024,768]{1,0:T(8,128)(2,1)}) %all-gather.17.cloned.1.call-update) | async-done | bytes 1572880 | tf_op jit(solution)/shard_map/all_gather | solution.py:142
  161.4 10.7 add_bitcast_fusion.2
  172.1 21.0 %all-gather.21.cloned.1.call-done = bf16[1,768,768]{1,2,0:T(8,128)(2,1)} async-done(((bf16[1,768,192]{1,2,0:T(8,128)(2,1)}), bf16[1,768,768]{1,2,0:T(8,128)(2,1)}) %all-gather.21.cloned.1.call-update) | async-done | bytes 1179664 | tf_op jit(solution)/shard_map/all_gather | solution.py:312
  197.6 30.2 %reduce-scatter.39.cloned.1.call-done = bf16[256,768]{1,0:T(8,128)(2,1)} async-done(((bf16[1024,768]{1,0:T(8,128)(2,1)}), bf16[256,768]{1,0:T(8,128)(2,1)}) %reduce-scatter.39.cloned.1.call-update) | async-done | bytes 393232 | tf_op jit(solution)/shard_map/reduce_scatter | solution.py:148
  236.1 29.2 %all-gather.23.cloned.1.call-done = bf16[1024,768]{1,0:T(8,128)(2,1)} async-done(((bf16[256,768]{1,0:T(8,128)(2,1)}), bf16[1024,768]{1,0:T(8,128)(2,1)}) %all-gather.23.cloned.1.call-update) | async-done | bytes 1572880 | tf_op jit(solution)/shard_map/all_gather | solution.py:118
  268.2 14.0 while.88
  285.8 30.5 %reduce-scatter.41.cloned.1.call-done = bf16[256,768]{1,0:T(8,128)(2,1)} async-done(((bf16[1024,768]{1,0:T(8,128)(2,1)}), bf16[256,768]{1,0:T(8,128)(2,1)}) %reduce-scatter.41.cloned.1.call-update) | async-done | bytes 393232 | tf_op jit(solution)/shard_map/reduce_scatter | solution.py:133
  321.7 31.1 %all-gather.25.cloned.1.call-done = bf16[1024,768]{1,0:T(8,128)(2,1)} async-done(((bf16[256,768]{1,0:T(8,128)(2,1)}), bf16[1024,768]{1,0:T(8,128)(2,1)}) %all-gather.25.cloned.1.call-update) | async-done | bytes 1572880 | tf_op jit(solution)/shard_map/all_gather | solution.py:142
  352.8 10.4 add_bitcast_fusion.1
  368.3 31.0 %reduce-scatter.43.cloned.1.call-done = bf16[256,768]{1,0:T(8,128)(2,1)} async-done(((bf16[1024,768]{1,0:T(8,128)(2,1)}), bf16[256,768]{1,0:T(8,128)(2,1)}) %reduce-scatter.43.cloned.1.call-update) | async-done | bytes 393232 | tf_op jit(solution)/shard_map/reduce_scatter | solution.py:148
  407.7 29.3 %all-gather.27.cloned.1.call-done = bf16[1024,768]{1,0:T(8,128)(2,1)} async-done(((bf16[256,768]{1,0:T(8,128)(2,1)}), bf16[1024,768]{1,0:T(8,128)(2,1)}) %all-gather.27.cloned.1.call-update) | async-done | bytes 1572880 | tf_op jit(solution)/shard_map/all_gather | solution.py:118
  439.9 14.1 while.89
  457.4 30.9 %reduce-scatter.45.cloned.1.call-done = bf16[256,768]{1,0:T(8,128)(2,1)} async-done(((bf16[1024,768]{1,0:T(8,128)(2,1)}), bf16[256,768]{1,0:T(8,128)(2,1)}) %reduce-scatter.45.cloned.1.call-update) | async-done | bytes 393232 | tf_op jit(solution)/shard_map/reduce_scatter | solution.py:133
  497.7 27.0 %all-gather.29.cloned.1.call-done = bf16[1024,768]{1,0:T(8,128)(2,1)} async-done(((bf16[256,768]{1,0:T(8,128)(2,1)}), bf16[1024,768]{1,0:T(8,128)(2,1)}) %all-gather.29.cloned.1.call-update) | async-done | bytes 1572880 | tf_op jit(solution)/shard_map/all_gather | solution.py:142
  524.7 10.2 add_bitcast_fusion
  534.9 7.2 pad_maximum_fusion
  542.0 15.5 %all-gather.31.cloned.1.call-done = bf16[1024,768]{1,0:T(8,128)(2,1)} async-done(((bf16[256,768]{1,0:T(8,128)(2,1)}), bf16[1024,768]{1,0:T(8,128)(2,1)}) %all-gather.31.cloned.1.call-update) | async-done | bytes 1572880 | tf_op jit(solution)/shard_map/all_gather | solution.py:207
  557.6 10.5 convert_reduce_fusion.2
  575.3 27.6 %reduce-scatter.49.cloned.1.call-done = bf16[256,768]{1,0:T(8,128)(2,1)} async-done(((bf16[1024,768]{1,0:T(8,128)(2,1)}), bf16[256,768]{1,0:T(8,128)(2,1)}) %reduce-scatter.49.cloned.1.call-update) | async-done | bytes 393232 | tf_op jit(solution)/shard_map/reduce_scatter | solution.py:217
  619.5 22.3 %all-gather.33.cloned.1.call-done = bf16[1024,768]{1,0:T(8,128)(2,1)} async-done(((bf16[256,768]{1,0:T(8,128)(2,1)}), bf16[1024,768]{1,0:T(8,128)(2,1)}) %all-gather.33.cloned.1.call-update) | async-done | bytes 1572880 | tf_op jit(solution)/shard_map/all_gather | solution.py:229
  644.7 28.5 %while.90 = (s32[]{:T(128)}, f32[1024,3,64]{0,2,1:T(8,128)S(1)}, f32[1024,3,64]{0,2,1:T(8,128)S(1)}, bf16[2,512,3,64]{1,3,2,0:T(8,128)(2,1)}, s32[2]{0:T(128)S(1...) while((s32[]{:T(128)}, f32[1024,3,64]{0,2,1:T(8,128)S(1)}, ...), condition=%wide.region_43.44_spmd.clone, body=%wide.region_41.43_spmd.clone.sunk | while | flops 1023147008 | bytes 61667764 | solution.py:95
  679.8 30.9 %reduce-scatter.51.cloned.1.call-done = bf16[256,768]{1,0:T(8,128)(2,1)} async-done(((bf16[1024,768]{1,0:T(8,128)(2,1)}), bf16[256,768]{1,0:T(8,128)(2,1)}) %reduce-scatter.51.cloned.1.call-update) | async-done | bytes 393232 | tf_op jit(solution)/shard_map/reduce_scatter | solution.py:253
  722.1 30.7 %all-gather.35.cloned.1.call-done = bf16[1024,768]{1,0:T(8,128)(2,1)} async-done(((bf16[256,768]{1,0:T(8,128)(2,1)}), bf16[1024,768]{1,0:T(8,128)(2,1)}) %all-gather.35.cloned.1.call-update) | async-done | bytes 1572880 | tf_op jit(solution)/shard_map/all_gather | solution.py:207
  752.7 10.8 convert_reduce_fusion.1
  768.9 30.9 %reduce-scatter.53.cloned.1.call-done = bf16[256,768]{1,0:T(8,128)(2,1)} async-done(((bf16[1024,768]{1,0:T(8,128)(2,1)}), bf16[256,768]{1,0:T(8,128)(2,1)}) %reduce-scatter.53.cloned.1.call-update) | async-done | bytes 393232 | tf_op jit(solution)/shard_map/reduce_scatter | solution.py:217
  807.9 30.9 %all-gather.37.cloned.1.call-done = bf16[1024,768]{1,0:T(8,128)(2,1)} async-done(((bf16[256,768]{1,0:T(8,128)(2,1)}), bf16[1024,768]{1,0:T(8,128)(2,1)}) %all-gather.37.cloned.1.call-update) | async-done | bytes 1572880 | tf_op jit(solution)/shard_map/all_gather | solution.py:229
  841.7 28.2 %while.91 = (s32[]{:T(128)}, f32[1024,3,64]{0,2,1:T(8,128)S(1)}, f32[1024,3,64]{0,2,1:T(8,128)S(1)}, bf16[2,512,3,64]{1,3,2,0:T(8,128)(2,1)}, s32[2]{0:T(128)S(1...) while((s32[]{:T(128)}, f32[1024,3,64]{0,2,1:T(8,128)S(1)}, ...), condition=%wide.region_56.57_spmd.clone, body=%wide.region_54.56_spmd.clone.sunk | while | flops 1023147008 | bytes 60094880 | solution.py:95
  877.2 30.3 %reduce-scatter.55.cloned.1.call-done = bf16[256,768]{1,0:T(8,128)(2,1)} async-done(((bf16[1024,768]{1,0:T(8,128)(2,1)}), bf16[256,768]{1,0:T(8,128)(2,1)}) %reduce-scatter.55.cloned.1.call-update) | async-done | bytes 393232 | tf_op jit(solution)/shard_map/reduce_scatter | solution.py:253
  920.5 30.6 %all-gather.39.cloned.1.call-done = bf16[1024,768]{1,0:T(8,128)(2,1)} async-done(((bf16[256,768]{1,0:T(8,128)(2,1)}), bf16[1024,768]{1,0:T(8,128)(2,1)}) %all-gather.39.cloned.1.call-update) | async-done | bytes 1572880 | tf_op jit(solution)/shard_map/all_gather | solution.py:207
  951.2 10.8 convert_reduce_fusion
  967.3 30.9 %reduce-scatter.57.cloned.1.call-done = bf16[256,768]{1,0:T(8,128)(2,1)} async-done(((bf16[1024,768]{1,0:T(8,128)(2,1)}), bf16[256,768]{1,0:T(8,128)(2,1)}) %reduce-scatter.57.cloned.1.call-update) | async-done | bytes 393232 | tf_op jit(solution)/shard_map/reduce_scatter | solution.py:217
  1073.0 28.4 %while.92 = (s32[]{:T(128)}, f32[1024,3,64]{0,2,1:T(8,128)S(1)}, f32[1024,3,64]{0,2,1:T(8,128)S(1)}, bf16[2,512,3,64]{1,3,2,0:T(8,128)(2,1)}, s32[2]{0:T(128)S(1...) while((s32[]{:T(128)}, f32[1024,3,64]{0,2,1:T(8,128)S(1)}, ...), condition=%wide.region_69.70_spmd.clone, body=%wide.region_67.69_spmd.clone.sunk | while | flops 1023147008 | bytes 60094880 | solution.py:95
  1129.1 12.7 reduce-scatter.81.cloned.1.call-done
  1142.8 25.7 %reduce-scatter.75.cloned.1.call-done = bf16[192,576]{1,0:T(8,128)(2,1)} async-done(((bf16[768,576]{1,0:T(8,128)(2,1)}), bf16[192,576]{1,0:T(8,128)(2,1)}) %reduce-scatter.75.cloned.1.call-update) | async-done | bytes 221200
  1172.6 25.9 %reduce-scatter.61.cloned.1.call-done = bf16[192,768]{1,0:T(8,128)(2,1)} async-done(((bf16[768,768]{1,0:T(8,128)(2,1)}), bf16[192,768]{1,0:T(8,128)(2,1)}) %reduce-scatter.61.cloned.1.call-update) | async-done | bytes 294928 | tf_op jit(solution)/shard_map/reduce_scatter | solution.py:380
  1198.5 30.2 %reduce-scatter.63.cloned.1.call-done = bf16[192,768]{1,0:T(8,128)(2,1)} async-done(((bf16[768,768]{1,0:T(8,128)(2,1)}), bf16[192,768]{1,0:T(8,128)(2,1)}) %reduce-scatter.63.cloned.1.call-update) | async-done | bytes 294928 | tf_op jit(solution)/shard_map/reduce_scatter | solution.py:380
  1228.7 30.1 %reduce-scatter.65.cloned.1.call-done = bf16[192,768]{1,0:T(8,128)(2,1)} async-done(((bf16[768,768]{1,0:T(8,128)(2,1)}), bf16[192,768]{1,0:T(8,128)(2,1)}) %reduce-scatter.65.cloned.1.call-update) | async-done | bytes 294928 | tf_op jit(solution)/shard_map/reduce_scatter | solution.py:380
  1260.9 28.2 %reduce-scatter.67.cloned.1.call-done = bf16[768,192]{0,1:T(8,128)(2,1)} async-done(((bf16[768,768]{0,1:T(8,128)(2,1)}), bf16[768,192]{0,1:T(8,128)(2,1)}) %reduce-scatter.67.cloned.1.call-update) | async-done | bytes 294928 | tf_op jit(solution)/shard_map/reduce_scatter | solution.py:383
  1289.1 30.2 %reduce-scatter.69.cloned.1.call-done = bf16[768,192]{0,1:T(8,128)(2,1)} async-done(((bf16[768,768]{0,1:T(8,128)(2,1)}), bf16[768,192]{0,1:T(8,128)(2,1)}) %reduce-scatter.69.cloned.1.call-update) | async-done | bytes 294928 | tf_op jit(solution)/shard_map/reduce_scatter | solution.py:383
  1319.3 30.2 %reduce-scatter.71.cloned.1.call-done = bf16[768,192]{0,1:T(8,128)(2,1)} async-done(((bf16[768,768]{0,1:T(8,128)(2,1)}), bf16[768,192]{0,1:T(8,128)(2,1)}) %reduce-scatter.71.cloned.1.call-update) | async-done | bytes 294928 | tf_op jit(solution)/shard_map/reduce_scatter | solution.py:383
  1353.8 17.2 %reduce-scatter.83.cloned.1.call-done = bf16[192,192]{1,0:T(8,128)(2,1)} async-done(((bf16[768,192]{1,0:T(8,128)(2,1)}), bf16[192,192]{1,0:T(8,128)(2,1)}) %reduce-scatter.83.cloned.1.call-update) | async-done | bytes 73744
  1372.7 25.2 %reduce-scatter.77.cloned.1.call-done = bf16[192,576]{1,0:T(8,128)(2,1)} async-done(((bf16[768,576]{1,0:T(8,128)(2,1)}), bf16[192,576]{1,0:T(8,128)(2,1)}) %reduce-scatter.77.cloned.1.call-update) | async-done | bytes 221200
  1404.3 26.0 %reduce-scatter.59.cloned.1.call-done = bf16[256,768]{1,0:T(8,128)(2,1)} async-done(((bf16[1024,768]{1,0:T(8,128)(2,1)}), bf16[256,768]{1,0:T(8,128)(2,1)}) %reduce-scatter.59.cloned.1.call-update) | async-done | bytes 393232 | tf_op jit(solution)/shard_map/reduce_scatter | solution.py:253
  1436.4 76.4 %all-reduce = (f32[1,2,768]{2,1,0:T(2,128)}, f32[1,2,768]{2,1,0:T(2,128)}, f32[2,768]{1,0:T(2,128)}, f32[1,768]{1,0:T(1,128)}, f32[3072]{0:T(1024)}, /*index=5*/f32[1,768]{1,0:T(1,128)}) all-reduce(f32[1,2,768]{2,1,0:T(2,128)} %fusion.378, f32[1,2,768]{2,1,0:T(2,128)} %fusion.380, ...), channel_id=1, replica_groups=mesh['section'=2,'dp'=4,'tensor'=4] {'dp','tensor'}, use_global_device_ids=true, to_apply=%region_81.82 | all-reduce | flops 9216 | bytes 73728 | tf_op jit(solution)/shard_map/psum | solution.py:402
  (867 shorter events, 408.9 us)
Async XLA Ops:
  8.0 61.0 %all-gather.15.cloned.1.call-start = ((), (), s32[]{:S(2)}) async-start(), calls=%async_computation.24 | async-start | bytes 1966080 | tf_op jit(solution)/shard_map/all_gather | solution.py:118
  11.3 393.8 %copy-start.102 = (f32[768]{0:T(1024)}, f32[768]{0:T(1024)S(1)}, u32[]{:S(2)}) copy-start(f32[768]{0:T(1024)S(1)} %get-tuple-element.586) | copy-start | bytes 9220
  11.3 595.6 %copy-start.108 = (f32[768]{0:T(1024)}, f32[768]{0:T(1024)S(1)}, u32[]{:S(2)}) copy-start(f32[768]{0:T(1024)S(1)} %get-tuple-element.585) | copy-start | bytes 9220
  14.0 111.0 %reduce-scatter.37.cloned.1.call-start = ((), (), s32[]{:S(2)}) async-start(), calls=%async_computation.25 | async-start | bytes 1966080 | tf_op jit(solution)/shard_map/reduce_scatter | solution.py:133
  40.2 415.0 %copy-start.44 = (bf16[1,192,768]{2,1,0:T(8,128)(2,1)}, bf16[1,192,768]{2,1,0:T(8,128)(2,1)S(1)}, u32[]{:S(2)}) copy-start(bf16[1,192,768]{2,1,0:T(8,128)(2,1)S(1)} %copy.68) | copy-start | bytes 884740
  92.9 38.4 %all-gather.19.cloned.1.call-start = ((), (), s32[]{:S(2)}) async-start(), calls=%async_computation.27 | async-start | bytes 1474560 | tf_op jit(solution)/shard_map/all_gather | solution.py:311
  93.5 67.9 %all-gather.17.cloned.1.call-start = ((), (), s32[]{:S(2)}) async-start(), calls=%async_computation.26 | async-start | bytes 1966080 | tf_op jit(solution)/shard_map/all_gather | solution.py:142
  93.6 398.0 %copy-start.106 = (f32[768]{0:T(1024)}, f32[768]{0:T(1024)S(1)}, u32[]{:S(2)}) copy-start(f32[768]{0:T(1024)S(1)} %reduce.15) | copy-start | bytes 9220
  130.5 62.6 %all-gather.21.cloned.1.call-start = ((), (), s32[]{:S(2)}) async-start(), calls=%async_computation.28 | async-start | bytes 1474560 | tf_op jit(solution)/shard_map/all_gather | solution.py:312
  131.1 96.7 %reduce-scatter.39.cloned.1.call-start = ((), (), s32[]{:S(2)}) async-start(), calls=%async_computation.29 | async-start | bytes 1966080 | tf_op jit(solution)/shard_map/reduce_scatter | solution.py:148
  197.5 67.9 %all-gather.23.cloned.1.call-start = ((), (), s32[]{:S(2)}) async-start(), calls=%async_computation.30 | async-start | bytes 1966080 | tf_op jit(solution)/shard_map/all_gather | solution.py:118
  229.0 3.1 collective-permute-start
  234.5 81.8 %reduce-scatter.41.cloned.1.call-start = ((), (), s32[]{:S(2)}) async-start(), calls=%async_computation.31 | async-start | bytes 1966080 | tf_op jit(solution)/shard_map/reduce_scatter | solution.py:133
  285.4 67.4 %all-gather.25.cloned.1.call-start = ((), (), s32[]{:S(2)}) async-start(), calls=%async_computation.32 | async-start | bytes 1966080 | tf_op jit(solution)/shard_map/all_gather | solution.py:142
  321.6 77.7 %reduce-scatter.43.cloned.1.call-start = ((), (), s32[]{:S(2)}) async-start(), calls=%async_computation.33 | async-start | bytes 1966080 | tf_op jit(solution)/shard_map/reduce_scatter | solution.py:148
  368.3 68.7 %all-gather.27.cloned.1.call-start = ((), (), s32[]{:S(2)}) async-start(), calls=%async_computation.34 | async-start | bytes 1966080 | tf_op jit(solution)/shard_map/all_gather | solution.py:118
  400.6 3.1 collective-permute-start.1
  406.1 82.2 %reduce-scatter.45.cloned.1.call-start = ((), (), s32[]{:S(2)}) async-start(), calls=%async_computation.35 | async-start | bytes 1966080 | tf_op jit(solution)/shard_map/reduce_scatter | solution.py:133
  457.3 67.4 %all-gather.29.cloned.1.call-start = ((), (), s32[]{:S(2)}) async-start(), calls=%async_computation.36 | async-start | bytes 1966080 | tf_op jit(solution)/shard_map/all_gather | solution.py:142
  493.6 64.0 %all-gather.31.cloned.1.call-start = ((), (), s32[]{:S(2)}) async-start(), calls=%async_computation.38 | async-start | bytes 1966080 | tf_op jit(solution)/shard_map/all_gather | solution.py:207
  497.5 105.3 %reduce-scatter.49.cloned.1.call-start = ((), (), s32[]{:S(2)}) async-start(), calls=%async_computation.39 | async-start | bytes 1966080 | tf_op jit(solution)/shard_map/reduce_scatter | solution.py:217
  571.9 70.0 %all-gather.33.cloned.1.call-start = ((), (), s32[]{:S(2)}) async-start(), calls=%async_computation.40 | async-start | bytes 1966080 | tf_op jit(solution)/shard_map/all_gather | solution.py:229
  610.7 100.0 %reduce-scatter.51.cloned.1.call-start = ((), (), s32[]{:S(2)}) async-start(), calls=%async_computation.41 | async-start | bytes 1966080 | tf_op jit(solution)/shard_map/reduce_scatter | solution.py:253
  679.7 73.0 %all-gather.35.cloned.1.call-start = ((), (), s32[]{:S(2)}) async-start(), calls=%async_computation.42 | async-start | bytes 1966080 | tf_op jit(solution)/shard_map/all_gather | solution.py:207
  716.3 3.6 collective-permute-start.2
  721.6 78.1 %reduce-scatter.53.cloned.1.call-start = ((), (), s32[]{:S(2)}) async-start(), calls=%async_computation.43 | async-start | bytes 1966080 | tf_op jit(solution)/shard_map/reduce_scatter | solution.py:217
  768.8 70.0 %all-gather.37.cloned.1.call-start = ((), (), s32[]{:S(2)}) async-start(), calls=%async_computation.44 | async-start | bytes 1966080 | tf_op jit(solution)/shard_map/all_gather | solution.py:229
  807.7 99.9 %reduce-scatter.55.cloned.1.call-start = ((), (), s32[]{:S(2)}) async-start(), calls=%async_computation.45 | async-start | bytes 1966080 | tf_op jit(solution)/shard_map/reduce_scatter | solution.py:253
  876.4 74.7 %all-gather.39.cloned.1.call-start = ((), (), s32[]{:S(2)}) async-start(), calls=%async_computation.46 | async-start | bytes 1966080 | tf_op jit(solution)/shard_map/all_gather | solution.py:207
  913.8 3.8 collective-permute-start.3
  920.2 77.9 %reduce-scatter.57.cloned.1.call-start = ((), (), s32[]{:S(2)}) async-start(), calls=%async_computation.47 | async-start | bytes 1966080 | tf_op jit(solution)/shard_map/reduce_scatter | solution.py:217
  967.2 102.9 %all-gather.41.cloned.1.call-start = ((), (), s32[]{:S(2)}) async-start(), calls=%async_computation.48 | async-start | bytes 1966080 | tf_op jit(solution)/shard_map/all_gather | solution.py:229
  1005.9 114.8 %reduce-scatter.47.cloned.1.call-start = ((), (), s32[]{:S(2)}) async-start(), calls=%async_computation.37 | async-start | bytes 1966080 | tf_op jit(solution)/shard_map/reduce_scatter | solution.py:148
  1010.4 113.0 %reduce-scatter.79.cloned.1.call-start = ((), (), s32[]{:S(2)}) async-start(), calls=%async_computation.59 | async-start | bytes 491520
  1015.4 109.1 %reduce-scatter.73.cloned.1.call-start = ((), (), s32[]{:S(2)}) async-start(), calls=%async_computation.56 | async-start | bytes 1228800
  1027.2 114.5 %reduce-scatter.81.cloned.1.call-start = ((), (), s32[]{:S(2)}) async-start(), calls=%async_computation.60 | async-start | bytes 491520
  1030.6 137.9 %reduce-scatter.75.cloned.1.call-start = ((), (), s32[]{:S(2)}) async-start(), calls=%async_computation.57 | async-start | bytes 1228800
  1039.1 159.4 %reduce-scatter.61.cloned.1.call-start = ((), (), s32[]{:S(2)}) async-start(), calls=%async_computation.50 | async-start | bytes 1474560 | tf_op jit(solution)/shard_map/reduce_scatter | solution.py:380
  1046.0 182.7 %reduce-scatter.63.cloned.1.call-start = ((), (), s32[]{:S(2)}) async-start(), calls=%async_computation.51 | async-start | bytes 1474560 | tf_op jit(solution)/shard_map/reduce_scatter | solution.py:380
  1050.1 208.7 %reduce-scatter.65.cloned.1.call-start = ((), (), s32[]{:S(2)}) async-start(), calls=%async_computation.52 | async-start | bytes 1474560 | tf_op jit(solution)/shard_map/reduce_scatter | solution.py:380
  1054.8 234.3 %reduce-scatter.67.cloned.1.call-start = ((), (), s32[]{:S(2)}) async-start(), calls=%async_computation.53 | async-start | bytes 1474560 | tf_op jit(solution)/shard_map/reduce_scatter | solution.py:383
  1061.4 257.9 %reduce-scatter.69.cloned.1.call-start = ((), (), s32[]{:S(2)}) async-start(), calls=%async_computation.54 | async-start | bytes 1474560 | tf_op jit(solution)/shard_map/reduce_scatter | solution.py:383
  1065.3 284.2 %reduce-scatter.71.cloned.1.call-start = ((), (), s32[]{:S(2)}) async-start(), calls=%async_computation.55 | async-start | bytes 1474560 | tf_op jit(solution)/shard_map/reduce_scatter | solution.py:383
  1069.9 301.2 %reduce-scatter.83.cloned.1.call-start = ((), (), s32[]{:S(2)}) async-start(), calls=%async_computation.61 | async-start | bytes 491520
  1105.2 292.7 %reduce-scatter.77.cloned.1.call-start = ((), (), s32[]{:S(2)}) async-start(), calls=%async_computation.58 | async-start | bytes 1228800
  1114.6 315.7 %reduce-scatter.59.cloned.1.call-start = ((), (), s32[]{:S(2)}) async-start(), calls=%async_computation.49 | async-start | bytes 1966080 | tf_op jit(solution)/shard_map/reduce_scatter | solution.py:253
  1123.2 229.6 %copy-start.147 = (f32[768]{0:T(1024)S(1)}, f32[768]{0:T(1024)}, u32[]{:S(2)}) copy-start(f32[768]{0:T(1024)} %get-tuple-element.723) | copy-start | bytes 9220
  1123.2 229.6 %copy-start.148 = (f32[768]{0:T(1024)S(1)}, f32[768]{0:T(1024)}, u32[]{:S(2)}) copy-start(f32[768]{0:T(1024)} %get-tuple-element.721) | copy-start | bytes 9220
  (187 other events, 4861.5 us)
Sparse Core Ops, SparseCore 0:
  14.2 33.7 all-gather.14
  93.0 32.0 reduce-scatter.36
  197.6 30.1 reduce-scatter.38
  321.8 30.9 all-gather.24
  368.4 30.9 reduce-scatter.42
  493.7 30.9 all-gather.28
  526.5 30.9 all-gather.30
  610.9 30.9 all-gather.32
  721.7 30.9 all-gather.34
  807.8 30.9 all-gather.36
  876.6 30.9 reduce-scatter.54
  1006.0 30.9 all-gather.40
  1040.0 30.9 reduce-scatter.46
  1073.1 20.5 reduce-scatter.78
  1096.0 24.3 reduce-scatter.72
  1122.6 19.1 reduce-scatter.80
  1144.1 24.3 reduce-scatter.74
  1170.7 27.7 reduce-scatter.60
  1200.8 27.8 reduce-scatter.62
  1230.9 27.8 reduce-scatter.64
  1261.1 27.8 reduce-scatter.66
  1291.4 27.8 reduce-scatter.68
  1321.6 27.8 reduce-scatter.70
  1351.7 19.2 reduce-scatter.82
  1373.4 24.3 reduce-scatter.76
  1400.7 29.4 reduce-scatter.58
Sparse Core Ops, SparseCore 1:
  94.9 31.3 all-gather.18
  130.6 30.8 all-gather.16
  162.8 30.1 all-gather.20
  234.6 30.8 all-gather.22
  285.4 30.8 reduce-scatter.40
  406.2 30.8 all-gather.26
  457.4 30.8 reduce-scatter.44
  572.0 30.8 reduce-scatter.48
  679.8 30.8 reduce-scatter.50
  768.9 30.8 reduce-scatter.52
  920.3 30.8 all-gather.38
  967.3 30.8 reduce-scatter.56
where the time goes:
time: 1540 us; the launch traced here: 1530 us
  waiting for transfers between devices  893 us (58%)
  matrix products  232 us (15%)
  other arithmetic  139 us (9%)
  blocking collectives  125 us (8%)
  local copies, waits for them, and re-layouts  89.5 us (6%)
  loops' own time  19.9 us (1%)
  between operations  18.3 us (1%)
    reduce_scatter x3, waiting for transfers between devices, layer_forward(): lax.psum_scatter(jnp.dot(rows_here, out_weight, preferred_element_type=jn...  92.9 us
    reduce_scatter x3, waiting for transfers between devices, layer_backward(): lax.psum_scatter(jnp.einsum('rf,df->rd', rows_here, up_weight, preferred_...  89.4 us
    reduce_scatter x3, waiting for transfers between devices, shards(): lax.psum_scatter(matrices[3].astype(jnp.bfloat16), 'dp', scatter_dimensio...  88.7 us
    all_gather x3, waiting for transfers between devices, layer_forward(): gathered_mid = lax.all_gather(normed_mid, 'tensor', axis=0, tiled=True)  88.1 us
    reduce_scatter x3, waiting for transfers between devices, layer_backward(): lax.psum_scatter(jnp.einsum('re,de->rd', rows_here, qkv_cat, preferred_el...  87.2 us
    reduce_scatter x3, waiting for transfers between devices, shards(): lax.psum_scatter(matrices[2].astype(jnp.bfloat16), 'dp', scatter_dimensio...  86.2 us
    unnamed x44, waiting for transfers between devices  82.5 us
    all_gather x3, waiting for transfers between devices, layer_backward(): lax.all_gather(grad_out.astype(jnp.bfloat16), 'tensor', axis=0, tiled=True)  76.8 us
  transfers between devices with their start and end apart: 42, of which 36 were waited for; matrix products, arithmetic and copies ran while one was open for 12% of the time, Pallas kernels for 0%

commit v1 on v0

v1 whole, which is shorter than its diff:
```python
import functools

import jax
import jax.numpy as jnp
from jax import lax
from jax.experimental import pallas as pl
from jax.experimental.pallas import tpu as pltpu
from jax.sharding import PartitionSpec as P

HD = 64
BF = jnp.bfloat16
F32 = jnp.float32
VMEM = pl.BlockSpec(memory_space=pltpu.VMEM)
SMEM = pl.BlockSpec(memory_space=pltpu.SMEM)
MIB = 1 << 20

GAIN0, GAIN1, SHIFT0, SHIFT1, B_OUT, B_DOWN, B_UP, B_QV = range(8)


def nn(left, right):
    return lax.dot_general(left, right, (((1,), (0,)), ((), ())), preferred_element_type=F32)


def nt(left, right):
    return lax.dot_general(left, right, (((1,), (1,)), ((), ())), preferred_element_type=F32)


def tn(left, right):
    return lax.dot_general(left, right, (((0,), (0,)), ((), ())), preferred_element_type=F32)


def call(body, outs, args, specs=None, scratch=(), flops=0, bytes_accessed=0, vmem=32, name=None):
    return pl.pallas_call(
        body,
        out_shape=[jax.ShapeDtypeStruct(s, d) for s, d in outs],
        in_specs=specs if specs is not None else [VMEM] * len(args),
        out_specs=[VMEM] * len(outs),
        scratch_shapes=list(scratch),
        compiler_params=pltpu.CompilerParams(vmem_limit_bytes=vmem * MIB),
        cost_estimate=pl.CostEstimate(flops=flops, bytes_accessed=bytes_accessed, transcendentals=0),
        name=name,
    )(*args)


def swap(value, axis, by):
    count = lax.axis_size(axis)
    return lax.ppermute(value, axis, [(i, i ^ by) for i in range(count)])


def gather_rel(own):
    return [own] + [swap(own, "tensor", k) for k in range(1, lax.axis_size("tensor"))]


def scatter_rel(parts):
    return [parts[0]] + [swap(parts[k], "tensor", k) for k in range(1, len(parts))]


def row_norm(x):
    mean = jnp.mean(x, axis=-1, keepdims=True)
    centred = x - mean
    var = jnp.mean(centred * centred, axis=-1, keepdims=True)
    inv = lax.rsqrt(var + 1e-05)
    return centred * inv, inv


def norm_back(grad, xhat, inv, gain):
    gx = grad * gain
    m1 = jnp.mean(gx, axis=-1, keepdims=True)
    m2 = jnp.mean(gx * xhat, axis=-1, keepdims=True)
    return inv * (gx - m1 - xhat * m2)


def add_terms(refs):
    total = refs[0][...].astype(F32)
    for ref in refs[1:]:
        total = total + ref[...].astype(F32)
    return total


def first_norm_body(x, vec, out):
    xhat, _ = row_norm(x[...].astype(F32))
    out[...] = (xhat * vec[GAIN0 : GAIN0 + 1, :] + vec[SHIFT0 : SHIFT0 + 1, :]).astype(BF)


def mid_fwd_body(parts, *refs):
    x, vec = refs[:2]
    terms = refs[2 : 2 + parts]
    mid, out = refs[2 + parts :]
    h = x[...].astype(F32) + add_terms(terms) + vec[B_OUT : B_OUT + 1, :]
    mid[...] = h
    xhat, _ = row_norm(h)
    out[...] = (xhat * vec[GAIN1 : GAIN1 + 1, :] + vec[SHIFT1 : SHIFT1 + 1, :]).astype(BF)


def end_fwd_body(parts, *refs):
    mid, vec, vec_next = refs[:3]
    terms = refs[3 : 3 + parts]
    result, out = refs[3 + parts :]
    y = (mid[...] + add_terms(terms) + vec[B_DOWN : B_DOWN + 1, :]).astype(BF)
    result[...] = y
    xhat, _ = row_norm(y.astype(F32))
    out[...] = (xhat * vec_next[GAIN0 : GAIN0 + 1, :] + vec_next[SHIFT0 : SHIFT0 + 1, :]).astype(BF)


def last_fwd_body(parts, *refs):
    mid, vec = refs[:2]
    terms = refs[2 : 2 + parts]
    (result,) = refs[2 + parts :]
    result[...] = (mid[...] + add_terms(terms) + vec[B_DOWN : B_DOWN + 1, :]).astype(BF)


def mid_bwd_body(parts, *refs):
    g, mid, vec = refs[:3]
    terms = refs[3 : 3 + parts]
    grad_mid, grad_low, small = refs[3 + parts :]
    grad = g[...].astype(F32)
    back = add_terms(terms)
    xhat, inv = row_norm(mid[...])
    dh = grad + norm_back(back, xhat, inv, vec[GAIN1 : GAIN1 + 1, :])
    grad_mid[...] = dh
    grad_low[...] = dh.astype(BF)
    small[0:1, :] = jnp.sum(back * xhat, axis=0, keepdims=True)
    small[1:2, :] = jnp.sum(back, axis=0, keepdims=True)
    small[2:3, :] = jnp.sum(dh, axis=0, keepdims=True)
    small[3:4, :] = jnp.sum(grad, axis=0, keepdims=True)


def end_bwd_body(parts, *refs):
    grad_mid, x, vec = refs[:3]
    terms = refs[3 : 3 + parts]
    result, small = refs[3 + parts :]
    back = add_terms(terms)
    xhat, inv = row_norm(x[...].astype(F32))
    result[...] = (grad_mid[...] + norm_back(back, xhat, inv, vec[GAIN0 : GAIN0 + 1, :])).astype(BF)
    small[0:1, :] = jnp.sum(back * xhat, axis=0, keepdims=True)
    small[1:2, :] = jnp.sum(back, axis=0, keepdims=True)


def strip_mask(meta, slots, first, rows, cols):
    place = first + lax.broadcasted_iota(jnp.int32, (rows, 1), 0)
    start = jnp.zeros((rows, 1), jnp.int32)
    for s in range(slots):
        end = meta[1 + s]
        start = jnp.where(place >= end, end, start)
    start = jnp.where(place >= meta[slots], place, start)
    key = lax.broadcasted_iota(jnp.int32, (rows, cols), 1)
    return (key >= start) & (key <= place)


def attend_fwd_body(parts, slots, *refs):
    meta, wqkv, wout, vec = refs[:4]
    pieces = refs[4 : 4 + parts]
    outs = refs[4 + parts : 4 + 2 * parts]
    q, k, v, o, stat = refs[4 + 2 * parts :]
    rank = meta[0]
    block, width = pieces[0].shape[0], wqkv.shape[2]
    qb = vec[B_QV : B_QV + 1, :width]
    vb = vec[B_QV : B_QV + 1, width : 2 * width]
    for j in range(parts):
        rows = pl.ds(pl.multiple_of((rank ^ j) * block, block), block)
        a = pieces[j][...]
        q[rows, :] = ((nn(a, wqkv[0]) + qb) * (HD**-0.5)).astype(BF)
        k[rows, :] = nn(a, wqkv[1]).astype(BF)
        v[rows, :] = (nn(a, wqkv[2]) + vb).astype(BF)
    for i in range(parts):
        rows, cols = slice(i * block, (i + 1) * block), (i + 1) * block
        mask = strip_mask(meta, slots, i * block, block, cols)
        lane = lax.broadcasted_iota(jnp.int32, (block, 128), 1)
        stats = jnp.zeros((block, 128), F32)
        for h in range(width // HD):
            own = slice(h * HD, (h + 1) * HD)
            s = jnp.where(mask, nt(q[rows, own], k[:cols, own]), -1e9)
            top = jnp.max(s, axis=-1, keepdims=True)
            e = jnp.exp(s - top)
            total = jnp.sum(e, axis=-1, keepdims=True)
            p = (e * (1.0 / total)).astype(BF)
            o[rows, own] = nn(p, v[:cols, own]).astype(BF)
            stats = jnp.where(lane == h, top + jnp.log(total), stats)
        stat[rows, :] = stats
    for j in range(parts):
        rows = pl.ds(pl.multiple_of((rank ^ j) * block, block), block)
        outs[j][...] = nt(o[rows, :], wout[...]).astype(BF)


def attend_bwd_body(parts, slots, *refs):
    meta, wqkv, wout, q, k, v, stat = refs[:7]
    pieces = refs[7 : 7 + parts]
    outs = refs[7 + parts : 7 + 2 * parts]
    dq, dk, dv, small, do, dkf, dvf = refs[7 + 2 * parts :]
    rank = meta[0]
    block, width = pieces[0].shape[0], wqkv.shape[2]
    for j in range(parts):
        rows = pl.ds(pl.multiple_of((rank ^ j) * block, block), block)
        do[rows, :] = nn(pieces[j][...], wout[...]).astype(BF)
    for i in reversed(range(parts)):
        rows, cols = slice(i * block, (i + 1) * block), (i + 1) * block
        mask = strip_mask(meta, slots, i * block, block, cols)
        for h in range(width // HD):
            own = slice(h * HD, (h + 1) * HD)
            qh, kh, vh, doh = q[rows, own], k[:cols, own], v[:cols, own], do[rows, own]
            s = jnp.where(mask, nt(qh, kh), -1e9)
            p = jnp.exp(s - stat[rows, h : h + 1])
            dp = nt(doh, vh)
            inner = jnp.sum(dp * p, axis=-1, keepdims=True)
            ds = (p * (dp - inner)).astype(BF)
            dq[rows, own] = (nn(ds, kh).astype(BF).astype(F32) * (HD**-0.5)).astype(BF)
            dkh, dvh = tn(ds, qh), tn(p.astype(BF), doh)
            if i == parts - 1:
                dkf[h] = dkh
                dvf[h] = dvh
            else:
                dkf[h, :cols] += dkh
                dvf[h, :cols] += dvh
    for h in range(width // HD):
        own = slice(h * HD, (h + 1) * HD)
        dk[:, own] = dkf[h].astype(BF)
        dv[:, own] = dvf[h].astype(BF)
    small[0:1, :] = jnp.sum(dq[...].astype(F32), axis=0, keepdims=True)
    small[1:2, :] = jnp.sum(dv[...].astype(F32), axis=0, keepdims=True)
    for j in range(parts):
        rows = pl.ds(pl.multiple_of((rank ^ j) * block, block), block)
        outs[j][...] = (
            nt(dq[rows, :], wqkv[0]) + nt(dk[rows, :], wqkv[1]) + nt(dv[rows, :], wqkv[2])
        ).astype(BF)


def attend_weights_body(parts, *refs):
    meta, o, dq, dk, dv = refs[:5]
    normed = refs[5 : 5 + parts]
    grads = refs[5 + parts : 5 + 2 * parts]
    gqkv, gout = refs[5 + 2 * parts :]
    rank = meta[0]
    block = normed[0].shape[0]
    totals = [None] * 4
    for j in range(parts):
        rows = pl.ds(pl.multiple_of((rank ^ j) * block, block), block)
        a, g = normed[j][...], grads[j][...]
        terms = [tn(a, dq[rows, :]), tn(a, dk[rows, :]), tn(a, dv[rows, :]), tn(g, o[rows, :])]
        totals = [t if s is None else s + t for s, t in zip(totals, terms)]
    for n in range(3):
        gqkv[n] = totals[n].astype(BF)
    gout[...] = totals[3].astype(BF)


def feed_fwd_body(parts, *refs):
    wup, wdown, vec = refs[:3]
    pieces = refs[3 : 3 + parts]
    outs = refs[3 + parts : 3 + 2 * parts]
    hidden, slope = refs[3 + 2 * parts :]
    block = pieces[0].shape[0]
    bias = vec[B_UP : B_UP + 1, : wup.shape[1]]
    for j in range(parts):
        rows = slice(j * block, (j + 1) * block)
        u = nn(pieces[j][...], wup[...]) + bias
        share = 0.5 * (1.0 + lax.erf(u * (0.5**0.5)))
        f = (u * share).astype(BF)
        hidden[rows, :] = f
        slope[rows, :] = share + u * (jnp.exp(-0.5 * (u * u)) * 0.3989422804014327)
        outs[j][...] = nt(f, wdown[...]).astype(BF)


def feed_bwd_body(parts, *refs):
    wup, wdown, slope = refs[:3]
    pieces = refs[3 : 3 + parts]
    outs = refs[3 + parts : 3 + 2 * parts]
    du, small = refs[3 + 2 * parts :]
    block = pieces[0].shape[0]
    total = None
    for j in range(parts):
        rows = slice(j * block, (j + 1) * block)
        d = (nn(pieces[j][...], wdown[...]) * slope[rows, :]).astype(BF)
        du[rows, :] = d
        term = jnp.sum(d.astype(F32), axis=0, keepdims=True)
        total = term if total is None else total + term
        outs[j][...] = nt(d, wup[...]).astype(BF)
    small[...] = total


def feed_weights_body(parts, *refs):
    hidden, du = refs[:2]
    normed = refs[2 : 2 + parts]
    grads = refs[2 + parts : 2 + 2 * parts]
    gup, gdown = refs[2 + 2 * parts :]
    block = normed[0].shape[0]
    up = down = None
    for j in range(parts):
        rows = slice(j * block, (j + 1) * block)
        t_up, t_down = tn(normed[j][...], du[rows, :]), tn(grads[j][...], hidden[rows, :])
        up, down = (t_up, t_down) if up is None else (up + t_up, down + t_down)
    gup[...] = up.astype(BF)
    gdown[...] = down.astype(BF)


def gather_dp(shard, dim):
    count = lax.axis_size("dp")
    if count > 8:
        return lax.all_gather(shard, "dp", axis=dim, tiled=True)
    rank = lax.axis_index("dp")
    size = shard.shape[dim]
    whole = jnp.zeros(shard.shape[:dim] + (size * count,) + shard.shape[dim + 1 :], shard.dtype)
    for k in range(count):
        piece = shard if k == 0 else swap(shard, "dp", k)
        whole = lax.dynamic_update_slice_in_dim(whole, piece, (rank ^ k) * size, dim)
    return whole


def sum_to_owner(grad, layer, dim):
    count = lax.axis_size("dp")
    grad = grad.astype(F32) + lax.ppermute(grad, "section", [(1 - layer, layer)]).astype(F32)
    grad = grad.astype(BF)
    if count > 8:
        return lax.psum_scatter(grad, "dp", scatter_dimension=dim, tiled=True).astype(F32)
    rank = lax.axis_index("dp")
    size = grad.shape[dim] // count
    total = lax.dynamic_slice_in_dim(grad, rank * size, size, dim).astype(F32)
    for k in range(1, count):
        block = lax.dynamic_slice_in_dim(grad, (rank ^ k) * size, size, dim)
        pairs = [(layer * count + i, layer * count + (i ^ k)) for i in range(count)]
        total = total + lax.ppermute(block, ("section", "dp"), pairs).astype(F32)
    return total


def sum_small(value, axis):
    count = lax.axis_size(axis)
    if count > 8:
        return lax.psum(value, axis)
    total = value
    for k in range(1, count):
        total = total + swap(value, axis, k)
    return total


def shards(
    inputs,
    cotangent,
    seq_lengths,
    norm_gain,
    norm_shift,
    w_qkv,
    b_qv,
    w_out,
    b_out,
    w_up,
    b_up,
    w_down,
    b_down,
):
    section = lax.axis_index("section")
    rank = lax.axis_index("tensor")
    parts = lax.axis_size("tensor")
    own_first = section == 0
    rows, width = inputs.shape[1], inputs.shape[2]
    total_rows = rows * parts
    slots = seq_lengths.shape[2]
    heads = w_qkv.shape[3]
    units = w_up.shape[2]

    def by_layer(own, other):
        return jnp.where(own_first, own, other), jnp.where(own_first, other, own)

    def both_layers(own):
        return by_layer(own, swap(own, "section", 1))

    def pad(row):
        return jnp.pad(row.reshape(1, -1), ((0, 0), (0, width - row.size)))

    packed = jnp.concatenate(
        [norm_gain[0], norm_shift[0], b_out, b_down, pad(b_up[0]), pad(b_qv[0])], axis=0
    )
    vec = both_layers(packed)
    x0 = lax.dynamic_index_in_dim(inputs, section, 0, keepdims=False)
    (normed,) = call(first_norm_body, [((rows, width), BF)], [x0, vec[0]], name="norm_first")
    a0 = gather_rel(normed)
    wqkv = both_layers(gather_dp(w_qkv[0], 1))
    wout = both_layers(gather_dp(w_out[0].T, 0))
    wup = both_layers(gather_dp(w_up[0], 0))
    wdown = both_layers(gather_dp(w_down[0].T, 0))

    lengths = lax.dynamic_index_in_dim(seq_lengths[:, 0], section, 0, keepdims=False)
    ends = jnp.cumsum(lengths).astype(jnp.int32)
    meta = jnp.concatenate([rank.astype(jnp.int32)[None], ends])
    place = rank * rows + jnp.arange(rows, dtype=jnp.int32)
    valid = (place < ends[-1])[:, None]
    cot = lax.dynamic_index_in_dim(cotangent, section, 0, keepdims=False)
    grad1 = jnp.where(valid, cot, jnp.zeros_like(cot))
    block_out = [((rows, width), BF)] * parts
    tall = ((total_rows, heads), BF)

    def attend_fwd(layer, pieces):
        res = call(
            functools.partial(attend_fwd_body, parts, slots),
            block_out + [tall, tall, tall, tall, ((total_rows, 128), F32)],
            [meta, wqkv[layer], wout[layer], vec[layer], *pieces],
            specs=[SMEM] + [VMEM] * (3 + parts),
            flops=4 * 10**9,
            bytes_accessed=8 * 10**6,
            vmem=40,
            name="attend_fwd",
        )
        return res[:parts], res[parts:]

    def feed_fwd(layer, pieces):
        res = call(
            functools.partial(feed_fwd_body, parts),
            block_out + [((total_rows, units), BF), ((total_rows, units), F32)],
            [wup[layer], wdown[layer], vec[layer], *pieces],
            flops=4 * 10**9,
            bytes_accessed=12 * 10**6,
            vmem=40,
            name="feed_fwd",
        )
        return res[:parts], res[parts:]

    def mid_fwd(layer, x, terms):
        return call(
            functools.partial(mid_fwd_body, parts),
            [((rows, width), F32), ((rows, width), BF)],
            [x, vec[layer], *terms],
            name="mid_fwd",
        )

    out0, att0 = attend_fwd(0, a0)
    mid0, normed = mid_fwd(0, x0, scatter_rel(out0))
    c0 = gather_rel(normed)
    down0, feed0 = feed_fwd(0, c0)
    x1, normed = call(
        functools.partial(end_fwd_body, parts),
        [((rows, width), BF), ((rows, width), BF)],
        [mid0, vec[0], vec[1], *scatter_rel(down0)],
        name="end_fwd",
    )
    a1 = gather_rel(normed)
    out1, att1 = attend_fwd(1, a1)
    mid1, normed = mid_fwd(1, x1, scatter_rel(out1))
    c1 = gather_rel(normed)
    g1 = gather_rel(grad1)
    down1, feed1 = feed_fwd(1, c1)
    (x2,) = call(
        functools.partial(last_fwd_body, parts),
        [((rows, width), BF)],
        [mid1, vec[1], *scatter_rel(down1)],
        name="last_fwd",
    )

    def layer_back(layer, grad, g, x, a, att, mid, c, feed):
        q, k, v, o, stat = att
        hidden, slope = feed
        res = call(
            functools.partial(feed_bwd_body, parts),
            block_out + [((total_rows, units), BF), ((1, units), F32)],
            [wup[layer], wdown[layer], slope, *g],
            flops=3 * 10**9,
            bytes_accessed=12 * 10**6,
            vmem=40,
            name="feed_bwd",
        )
        terms, (du, small_up) = scatter_rel(res[:parts]), res[parts:]
        gup, gdown = call(
            functools.partial(feed_weights_body, parts),
            [((width, units), BF), ((width, units), BF)],
            [hidden, du, *c, *g],
            flops=3 * 10**9,
            bytes_accessed=10 * 10**6,
            vmem=40,
            name="feed_weights",
        )
        dmid, dlow, small_mid = call(
            functools.partial(mid_bwd_body, parts),
            [((rows, width), F32), ((rows, width), BF), ((4, width), F32)],
            [grad, mid, vec[layer], *terms],
            name="mid_bwd",
        )
        hb = gather_rel(dlow)
        res = call(
            functools.partial(attend_bwd_body, parts, slots),
            block_out + [tall, tall, tall, ((2, heads), F32)],
            [meta, wqkv[layer], wout[layer], q, k, v, stat, *hb],
            specs=[SMEM] + [VMEM] * (6 + parts),
            scratch=[
                pltpu.VMEM((total_rows, heads), BF),
                pltpu.VMEM((heads // HD, total_rows, HD), F32),
                pltpu.VMEM((heads // HD, total_rows, HD), F32),
            ],
            flops=8 * 10**9,
            bytes_accessed=8 * 10**6,
            vmem=40,
            name="attend_bwd",
        )
        terms, (dq, dk, dv, small_qv) = scatter_rel(res[:parts]), res[parts:]
        gqkv, gout = call(
            functools.partial(attend_weights_body, parts),
            [((3, width, heads), BF), ((width, heads), BF)],
            [meta, o, dq, dk, dv, *a, *hb],
            specs=[SMEM] + [VMEM] * (4 + 2 * parts),
            flops=2 * 10**9,
            bytes_accessed=6 * 10**6,
            vmem=40,
            name="attend_weights",
        )
        dx, small_end = call(
            functools.partial(end_bwd_body, parts),
            [((rows, width), BF), ((2, width), F32)],
            [dmid, x, vec[layer], *terms],
            name="end_bwd",
        )
        totals = (
            sum_to_owner(gdown, layer, 0),
            sum_to_owner(gup, layer, 0),
            sum_to_owner(gout, layer, 0),
            sum_to_owner(gqkv, layer, 1),
        )
        return dx, totals, (small_end, small_mid, small_up, small_qv)

    dx1, totals1, small1 = layer_back(1, grad1, g1, x1, a1, att1, mid1, c1, feed1)
    g0 = gather_rel(dx1)
    dx0, totals0, small0 = layer_back(0, dx1, g0, x0, a0, att0, mid0, c0, feed0)

    gdown, gup, gout, gqkv = [
        jnp.where(own_first, first, second) for first, second in zip(totals0, totals1)
    ]

    def collect(first, second):
        keep = jnp.where(own_first, first, second)
        came = swap(jnp.where(own_first, second, first), "section", 1)
        low, high = by_layer(keep, came)
        return jnp.stack([low, high])[None]

    layer_out = collect(x1, x2)
    input_grad = collect(dx0, dx1)

    def pack_small(small):
        end, mid, up, qv = small
        return jnp.concatenate([end, mid], axis=0), jnp.concatenate([pad(up), pad(qv)], axis=0)

    whole0, part0 = pack_small(small0)
    whole1, part1 = pack_small(small1)
    whole = sum_small(jnp.where(own_first, whole0, whole1), "tensor")
    whole_away = sum_small(jnp.where(own_first, whole1, whole0), "tensor")
    mine = jnp.concatenate([whole, jnp.where(own_first, part0, part1)], axis=0)
    away = jnp.concatenate([whole_away, jnp.where(own_first, part1, part0)], axis=0)
    mine = sum_small(mine + swap(away, "section", 1), "dp")
    return (
        layer_out,
        input_grad,
        jnp.stack([mine[0], mine[2]])[None],
        jnp.stack([mine[1], mine[3]])[None],
        gqkv[None],
        mine[7, : 2 * heads].reshape(1, 2, heads),
        gout.T[None],
        mine[4][None],
        gup[None],
        mine[6, :units][None],
        gdown.T[None],
        mine[5][None],
    )


def solution(mesh):
    in_specs = (
        P(None, ("dp", "tensor"), None),
        P(None, ("dp", "tensor"), None),
        P(None, "dp", None),
        P("section", None, None),
        P("section", None, None),
        P("section", None, "dp", "tensor"),
        P("section", None, "tensor"),
        P("section", "tensor", "dp"),
        P("section", None),
        P("section", "dp", "tensor"),
        P("section", "tensor"),
        P("section", "tensor", "dp"),
        P("section", None),
    )
    out_specs = (
        P("section", None, ("dp", "tensor"), None),
        P("section", None, ("dp", "tensor"), None),
        P("section", None, None),
        P("section", None, None),
        P("section", None, "dp", "tensor"),
        P("section", None, "tensor"),
        P("section", "tensor", "dp"),
        P("section", None),
        P("section", "dp", "tensor"),
        P("section", "tensor"),
        P("section", "tensor", "dp"),
        P("section", None),
    )
    return jax.shard_map(shards, mesh=mesh, in_specs=in_specs, out_specs=out_specs, check_vma=False)
```

time: 1540 us -> 593 us (0.39)
  waiting for transfers between devices: 893 us -> 227 us
  matrix products: 232 us -> 0 us
  starting transfers between devices: 10.3 us -> 179 us
  blocking collectives: 125 us -> 0 us
  other arithmetic: 139 us -> 33.9 us
  Pallas kernels: 0 us -> 81.2 us
  local copies, waits for them, and re-layouts: 89.5 us -> 63.5 us
  loops' own time: 19.9 us -> 0 us
  between operations: 18.3 us -> 2.63 us
    reduce_scatter x18 -> x0, waiting for transfers between devices: 506 us -> none  [the longest x3 92.9 us: layer_forward(): lax.psum_scatter(jnp.dot(rows_here, out_weight, preferred_element_type=jn...]
    all_gather x14 -> x0, waiting for transfers between devices: 298 us -> none  [the longest x3 88.1 us: layer_forward(): gathered_mid = lax.all_gather(normed_mid, 'tensor', axis=0, tiled=True)]
    dot_general x78 -> x0, matrix products: 232 us -> none  [the longest x3 32.1 us: layer_backward(): jnp.einsum('rd,fd->rf', grad_full, down_weight, preferred_element_type=jn...]
    ppermute x4 -> x109, waiting for transfers between devices: 7.45 us -> 227 us  [the longest x77 200 us: swap(): return lax.ppermute(value, axis, [(i, i ^ by) for i in range(count)])]
    ppermute x4 -> x109, starting transfers between devices: 6.12 us -> 179 us  [the longest x77 107 us: swap(): return lax.ppermute(value, axis, [(i, i ^ by) for i in range(count)])]
    unnamed x44 -> x0, waiting for transfers between devices: 82.5 us -> none
    pallas_call x0 -> x21, Pallas kernels: none -> 81.2 us  [call(): pl.pallas_call(body, out_shape=[jax.ShapeDtypeStruct(s, d) for s, d in ou...]
    psum x1 -> x0, blocking collectives: 76.4 us -> none  [shards(): lax.psum((gain_grad, shift_grad, out_bias_grad, down_bias_grad, qv_wide,...]
  transfers between devices with their start and end apart: 42 -> 109, of which waited for: 36 -> 47; matrix products, arithmetic and copies ran while one was open for 12% -> 12% of each run, Pallas kernels for 0% -> 11%
where the time goes in v1:
time: 593 us; the launch traced here: 588 us
  waiting for transfers between devices  227 us (38%)
  starting transfers between devices  179 us (30%)
  Pallas kernels  81.2 us (14%)
  local copies, waits for them, and re-layouts  63.5 us (11%)
  other arithmetic  33.9 us (6%)
    ppermute x77, waiting for transfers between devices, swap(): return lax.ppermute(value, axis, [(i, i ^ by) for i in range(count)])  200 us
    ppermute x77, starting transfers between devices, swap(): return lax.ppermute(value, axis, [(i, i ^ by) for i in range(count)])  107 us
    pallas_call x21, Pallas kernels, call(): pl.pallas_call(body, out_shape=[jax.ShapeDtypeStruct(s, d) for s, d in ou...  81.2 us
    ppermute x24, starting transfers between devices, sum_to_owner(): total = total + lax.ppermute(block, ('section', 'dp'), pairs).astype(F32)  59.9 us
    unnamed x262, local copies, waits for them, and re-layouts  27.7 us
    ppermute x24, waiting for transfers between devices, sum_to_owner(): total = total + lax.ppermute(block, ('section', 'dp'), pairs).astype(F32)  26.4 us
    dynamic_update_slice x17, local copies, waits for them, and re-layouts, gather_dp(): lax.dynamic_update_slice_in_dim(whole, piece, (rank ^ k) * size, dim)  13.2 us
    ppermute x8, starting transfers between devices, sum_to_owner(): lax.ppermute(grad, 'section', [(1 - layer, layer)]).astype(F32)  12.6 us
  transfers between devices with their start and end apart: 109, of which 47 were waited for; matrix products, arithmetic and copies ran while one was open for 12% of the time, Pallas kernels for 11%

profile of v1, /device:TPU:0, one launch (start us, length us, event | category | flops | bytes accessed | tf_op | source)
XLA Modules:
  0.0 587.9 jit_solution(6658250531764479112)
XLA Ops:
  1.7 4.1 collective-permute-start.6
  22.3 3.0 collective-permute-start.15
  25.3 14.5 %collective-permute-done.1 = bf16[3,192,192]{2,1,0:T(8,128)(2,1)S(1)} collective-permute-done((bf16[3,192,192]{2,1,0:T(8,128)(2,1)S(1)}, bf16[3,192,192]{2,1,0:T(8,128)(2,1)S(1)}, u32[]{:S(2)}, u32[]{:S(2)}) %collective-permute-start.1) | collective-permute-done | bytes 221216 | tf_op jit(solution)/shard_map/ppermute | solution.py:47
  43.6 16.9 %collective-permute-start.19 = (bf16[192,768]{1,0:T(8,128)(2,1)S(1)}, bf16[192,768]{1,0:T(8,128)(2,1)S(1)}, u32[]{:S(2)}, u32[]{:S(2)}) collective-permute-start(bf16[192,768]{1,0:T(8,128)(2,1)S(1)} %bitcast.61), channel_id=1, source_target_pairs={{0,4},{4,0},{8,12},{12,8},{1,5},{5,1},{9,13},{13,9},{2,6},{6,2},{1... | collective-permute-start | bytes 884744 | tf_op jit(solution)/shard_map/ppermute | solution.py:47
  75.0 10.3 %collective-permute-done.20 = bf16[192,768]{1,0:T(8,128)(2,1)S(1)} collective-permute-done((bf16[192,768]{1,0:T(8,128)(2,1)S(1)}, bf16[192,768]{1,0:T(8,128)(2,1)S(1)}, u32[]{:S(2)}, u32[]{:S(2)}) %collective-permute-start.20) | collective-permute-done | bytes 294944 | tf_op jit(solution)/shard_map/ppermute | solution.py:47
  99.7 8.5 %attend_fwd.2 = (bf16[256,768]{1,0:T(8,128)(2,1)S(1)}, bf16[256,768]{1,0:T(8,128)(2,1)S(1)}, bf16[256,768]{1,0:T(8,128)(2,1)S(1)}, bf16[256,768]{1,0:T(8,128)(2,...) custom-call(s32[9]{0:T(128)S(1)} %pad_add_fusion.refs_0_, ...), custom_call_target="tpu_custom_call" | custom-call | flops 4000000000 | bytes 8000000 | tf_op jit(solution)/shard_map/attend_fwd/pallas_call | solution.py:33
  112.6 8.5 %collective-permute-done.12.refs_3_ = bf16[256,768]{1,0:T(8,128)(2,1)S(1)} collective-permute-done((bf16[256,768]{1,0:T(8,128)(2,1)S(1)}, bf16[256,768]{1,0:T(8,128)(2,1)S(1)}, u32[]{:S(2)}, u32[]{:S(2)}) %collective-permute-start.12) | collective-permute-done | bytes 393248 | tf_op jit(solution)/shard_map/ppermute | solution.py:47
  121.1 7.3 %collective-permute-done.13.refs_4_ = bf16[256,768]{1,0:T(8,128)(2,1)S(1)} collective-permute-done((bf16[256,768]{1,0:T(8,128)(2,1)S(1)}, bf16[256,768]{1,0:T(8,128)(2,1)S(1)}, u32[]{:S(2)}, u32[]{:S(2)}) %collective-permute-start.13) | collective-permute-done | bytes 393248 | tf_op jit(solution)/shard_map/ppermute | solution.py:47
  135.4 3.3 broadcast_select_fusion.1
  138.6 3.3 collective-permute-done.25.refs_6_.refs_5_
  142.0 5.2 collective-permute-done.24.refs_5_.refs_4_
  147.8 3.2 feed_fwd.2
  156.2 8.6 %collective-permute-done.26.refs_4_ = bf16[256,768]{1,0:T(8,128)(2,1)S(1)} collective-permute-done((bf16[256,768]{1,0:T(8,128)(2,1)S(1)}, bf16[256,768]{1,0:T(8,128)(2,1)S(1)}, u32[]{:S(2)}, u32[]{:S(2)}) %collective-permute-start.26) | collective-permute-done | bytes 393248 | tf_op jit(solution)/shard_map/ppermute | solution.py:47
  164.8 7.4 %collective-permute-done.27.refs_5_ = bf16[256,768]{1,0:T(8,128)(2,1)S(1)} collective-permute-done((bf16[256,768]{1,0:T(8,128)(2,1)S(1)}, bf16[256,768]{1,0:T(8,128)(2,1)S(1)}, u32[]{:S(2)}, u32[]{:S(2)}) %collective-permute-start.27) | collective-permute-done | bytes 393248 | tf_op jit(solution)/shard_map/ppermute | solution.py:47
  176.7 9.5 %collective-permute-done.31.refs_7_.refs_8_ = bf16[256,768]{1,0:T(8,128)(2,1)S(1)} collective-permute-done((bf16[256,768]{1,0:T(8,128)(2,1)S(1)}, bf16[256,768]{1,0:T(8,128)(2,1)S(1)}, u32[]{:S(2)}, u32[]{:S(2)}) %collective-permute-start.31) | collective-permute-done | bytes 393248 | tf_op jit(solution)/shard_map/ppermute | solution.py:47
  186.2 5.1 collective-permute-done.30.refs_6_.refs_7_
  191.3 8.5 %attend_fwd.3 = (bf16[256,768]{1,0:T(8,128)(2,1)S(1)}, bf16[256,768]{1,0:T(8,128)(2,1)S(1)}, bf16[256,768]{1,0:T(8,128)(2,1)S(1)}, bf16[256,768]{1,0:T(8,128)(2,...) custom-call(s32[9]{0:T(128)S(1)} %pad_add_fusion.refs_0_, ...), custom_call_target="tpu_custom_call" | custom-call | flops 4000000000 | bytes 8000000 | tf_op jit(solution)/shard_map/attend_fwd/pallas_call | solution.py:33
  204.9 8.5 %collective-permute-done.32.refs_3_ = bf16[256,768]{1,0:T(8,128)(2,1)S(1)} collective-permute-done((bf16[256,768]{1,0:T(8,128)(2,1)S(1)}, bf16[256,768]{1,0:T(8,128)(2,1)S(1)}, u32[]{:S(2)}, u32[]{:S(2)}) %collective-permute-start.32) | collective-permute-done | bytes 393248 | tf_op jit(solution)/shard_map/ppermute | solution.py:47
  213.4 7.7 %collective-permute-done.34.refs_5_ = bf16[256,768]{1,0:T(8,128)(2,1)S(1)} collective-permute-done((bf16[256,768]{1,0:T(8,128)(2,1)S(1)}, bf16[256,768]{1,0:T(8,128)(2,1)S(1)}, u32[]{:S(2)}, u32[]{:S(2)}) %collective-permute-start.34) | collective-permute-done | bytes 393248 | tf_op jit(solution)/shard_map/ppermute | solution.py:47
  231.3 4.4 collective-permute-done.37.refs_6_.refs_5_
  237.2 11.8 %collective-permute-done.36.refs_5_.refs_4_ = bf16[256,768]{1,0:T(8,128)(2,1)} collective-permute-done((bf16[256,768]{1,0:T(8,128)(2,1)}, bf16[256,768]{1,0:T(8,128)(2,1)}, u32[]{:S(2)}, u32[]{:S(2)}) %collective-permute-start.36) | collective-permute-done | bytes 393248 | tf_op jit(solution)/shard_map/ppermute | solution.py:47
  251.5 4.5 feed_fwd.3
  266.3 7.6 %collective-permute-done.45.refs_4_ = bf16[256,768]{1,0:T(8,128)(2,1)S(1)} collective-permute-done((bf16[256,768]{1,0:T(8,128)(2,1)S(1)}, bf16[256,768]{1,0:T(8,128)(2,1)S(1)}, u32[]{:S(2)}, u32[]{:S(2)}) %collective-permute-start.45) | collective-permute-done | bytes 393248 | tf_op jit(solution)/shard_map/ppermute | solution.py:47
  274.2 8.2 %collective-permute-done.46.refs_5_ = bf16[256,768]{1,0:T(8,128)(2,1)S(1)} collective-permute-done((bf16[256,768]{1,0:T(8,128)(2,1)S(1)}, bf16[256,768]{1,0:T(8,128)(2,1)S(1)}, u32[]{:S(2)}, u32[]{:S(2)}) %collective-permute-start.46) | collective-permute-done | bytes 393248 | tf_op jit(solution)/shard_map/ppermute | solution.py:47
  287.5 3.3 collective-permute-done.38.refs_3_
  290.9 4.8 feed_weights.3
  295.8 11.9 %collective-permute-done.39.refs_4_ = bf16[256,768]{1,0:T(8,128)(2,1)S(1)} collective-permute-done((bf16[256,768]{1,0:T(8,128)(2,1)S(1)}, bf16[256,768]{1,0:T(8,128)(2,1)S(1)}, u32[]{:S(2)}, u32[]{:S(2)}) %collective-permute-start.39) | collective-permute-done | bytes 393248 | tf_op jit(solution)/shard_map/ppermute | solution.py:47
  310.4 4.5 collective-permute-done.49.refs_9_.refs_11_
  315.0 12.9 %attend_bwd.2 = (bf16[256,768]{1,0:T(8,128)(2,1)S(1)}, bf16[256,768]{1,0:T(8,128)(2,1)}, bf16[256,768]{1,0:T(8,128)(2,1)}, bf16[256,768]{1,0:T(8,128)(2,1)}, bf1...) custom-call(s32[9]{0:T(128)S(1)} %pad_add_fusion.refs_0_, ...), custom_call_target="tpu_custom_call" | custom-call | flops 8000000000 | bytes 8000000 | tf_op jit(solution)/shard_map/attend_bwd/pallas_call | solution.py:33
  329.4 3.6 attend_weights.3
  347.5 5.9 %collective-permute-done.52.refs_5_ = bf16[256,768]{1,0:T(8,128)(2,1)} collective-permute-done((bf16[256,768]{1,0:T(8,128)(2,1)}, bf16[256,768]{1,0:T(8,128)(2,1)}, u32[]{:S(2)}, u32[]{:S(2)}) %collective-permute-start.52) | collective-permute-done | bytes 393248 | tf_op jit(solution)/shard_map/ppermute | solution.py:47
  363.3 5.3 collective-permute-done.56.refs_6_.refs_9_
  368.6 4.5 collective-permute-done.55.refs_5_.refs_8_
  382.2 5.8 collective-permute-done.57.refs_4_
  388.0 7.7 %collective-permute-done.58.refs_5_ = bf16[256,768]{1,0:T(8,128)(2,1)S(1)} collective-permute-done((bf16[256,768]{1,0:T(8,128)(2,1)S(1)}, bf16[256,768]{1,0:T(8,128)(2,1)S(1)}, u32[]{:S(2)}, u32[]{:S(2)}) %collective-permute-start.58) | collective-permute-done | bytes 393248 | tf_op jit(solution)/shard_map/ppermute | solution.py:47
  412.5 4.0 collective-permute-done.61.refs_9_.refs_11_
  422.8 13.8 %attend_bwd.3 = (bf16[256,768]{1,0:T(8,128)(2,1)S(1)}, bf16[256,768]{1,0:T(8,128)(2,1)}, bf16[256,768]{1,0:T(8,128)(2,1)}, bf16[256,768]{1,0:T(8,128)(2,1)S(1)},...) custom-call(s32[9]{0:T(128)S(1)} %copy-done.74, ...), custom_call_target="tpu_custom_call" | custom-call | flops 8000000000 | bytes 8000000 | tf_op jit(solution)/shard_map/attend_bwd/pallas_call | solution.py:33
  437.4 3.6 attend_weights.2
  448.9 11.8 %collective-permute-start.86 = (bf16[192,192]{1,0:T(8,128)(2,1)S(1)}, bf16[192,192]{1,0:T(8,128)(2,1)S(1)}, u32[]{:S(2)}, u32[]{:S(2)}) collective-permute-start(bf16[192,192]{1,0:T(8,128)(2,1)S(1)} %get-tuple-element.230), channel_id=1, source_target_pairs={{0,4},{4,0},{8,12},{12,8},{1,5},{5,1},{9,13},{13,9},{2,6},{6,2},{1... | collective-permute-start | bytes 221192 | tf_op jit(solution)/shard_map/ppermute | solution.py:319
  460.8 5.3 collective-permute-start.88
  484.4 6.5 %collective-permute-done.64.refs_5_ = bf16[256,768]{1,0:T(8,128)(2,1)} collective-permute-done((bf16[256,768]{1,0:T(8,128)(2,1)}, bf16[256,768]{1,0:T(8,128)(2,1)}, u32[]{:S(2)}, u32[]{:S(2)}) %collective-permute-start.64) | collective-permute-done | bytes 393248 | tf_op jit(solution)/shard_map/ppermute | solution.py:47
  518.5 3.2 collective-permute-start.96
  521.7 3.2 collective-permute-start.95
  528.2 3.7 collective-permute-start.102
  531.9 3.2 collective-permute-start.104
  535.1 13.8 %collective-permute-done.95 = bf16[192,768]{1,0:T(8,128)(2,1)S(1)} collective-permute-done((bf16[192,768]{1,0:T(8,128)(2,1)S(1)}, bf16[192,768]{1,0:T(8,128)(2,1)S(1)}, u32[]{:S(2)}, u32[]{:S(2)}) %collective-permute-start.95) | collective-permute-done | bytes 294944 | tf_op jit(solution)/shard_map/ppermute | solution.py:319
  566.4 5.2 collective-permute-start.80
  577.9 7.4 %collective-permute-done.79 = bf16[3,192,192]{2,1,0:T(8,128)(2,1)S(1)} collective-permute-done((bf16[3,192,192]{2,1,0:T(8,128)(2,1)S(1)}, bf16[3,192,192]{2,1,0:T(8,128)(2,1)S(1)}, u32[]{:S(2)}, u32[]{:S(2)}) %collective-permute-start.79) | collective-permute-done | bytes 221216 | tf_op jit(solution)/shard_map/ppermute | solution.py:319
  (533 shorter events, 250.4 us)
Async XLA Ops:
  1.7 19.0 %collective-permute-start.6 = (bf16[192,192]{1,0:T(8,128)(2,1)S(1)}, bf16[192,192]{1,0:T(8,128)(2,1)S(1)}, u32[]{:S(2)}, u32[]{:S(2)}) collective-permute-start(bf16[192,192]{1,0:T(8,128)(2,1)S(1)} %bitcast.51), channel_id=1, source_target_pairs={{0,8},{4,12},{8,0},{12,4},{1,9},{5,13},{9,1},{13,5},{2,10},{6,14},... | collective-permute-start | bytes 221192 | tf_op jit(solution)/shard_map/ppermute | solution.py:47
  9.0 33.8 %collective-permute-start.2 = (bf16[3,192,192]{2,1,0:T(8,128)(2,1)}, bf16[3,192,192]{2,1,0:T(8,128)(2,1)S(1)}, u32[]{:S(2)}, u32[]{:S(2)}) collective-permute-start(bf16[3,192,192]{2,1,0:T(8,128)(2,1)} %bitcast.54), channel_id=1, source_target_pairs={{0,8},{4,12},{8,0},{12,4},{1,9},{5,13},{9,1},{13,5},{2,10},{6,14},... | collective-permute-start | bytes 663560 | tf_op jit(solution)/shard_map/ppermute | solution.py:47
  17.7 22.1 %collective-permute-start.1 = (bf16[3,192,192]{2,1,0:T(8,128)(2,1)S(1)}, bf16[3,192,192]{2,1,0:T(8,128)(2,1)S(1)}, u32[]{:S(2)}, u32[]{:S(2)}) collective-permute-start(bf16[3,192,192]{2,1,0:T(8,128)(2,1)S(1)} %bitcast.55), channel_id=1, source_target_pairs={{0,4},{4,0},{8,12},{12,8},{1,5},{5,1},{9,13},{13,9},{2,6},{6,2},{1... | collective-permute-start | bytes 663560 | tf_op jit(solution)/shard_map/ppermute | solution.py:47
  20.6 23.0 %collective-permute-start.3 = (bf16[3,192,192]{2,1,0:T(8,128)(2,1)S(1)}, bf16[3,192,192]{2,1,0:T(8,128)(2,1)S(1)}, u32[]{:S(2)}, u32[]{:S(2)}) collective-permute-start(bf16[3,192,192]{2,1,0:T(8,128)(2,1)S(1)} %bitcast.56), channel_id=1, source_target_pairs={{0,12},{4,8},{8,4},{12,0},{1,13},{5,9},{9,5},{13,1},{2,14},{6,10},... | collective-permute-start | bytes 663560 | tf_op jit(solution)/shard_map/ppermute | solution.py:47
  20.8 45.6 %collective-permute-start.16 = (bf16[192,768]{1,0:T(8,128)(2,1)S(1)}, bf16[192,768]{1,0:T(8,128)(2,1)S(1)}, u32[]{:S(2)}, u32[]{:S(2)}) collective-permute-start(bf16[192,768]{1,0:T(8,128)(2,1)S(1)} %bitcast.57), channel_id=1, source_target_pairs={{0,8},{4,12},{8,0},{12,4},{1,9},{5,13},{9,1},{13,5},{2,10},{6,14},... | collective-permute-start | bytes 884744 | tf_op jit(solution)/shard_map/ppermute | solution.py:47
  22.3 41.3 %collective-permute-start.15 = (bf16[192,768]{1,0:T(8,128)(2,1)S(1)}, bf16[192,768]{1,0:T(8,128)(2,1)}, u32[]{:S(2)}, u32[]{:S(2)}) collective-permute-start(bf16[192,768]{1,0:T(8,128)(2,1)S(1)} %bitcast.58), channel_id=1, source_target_pairs={{0,4},{4,0},{8,12},{12,8},{1,5},{5,1},{9,13},{13,9},{2,6},{6,2},{1... | collective-permute-start | bytes 884744 | tf_op jit(solution)/shard_map/ppermute | solution.py:47
  39.8 30.3 %collective-permute-start.17 = (bf16[192,768]{1,0:T(8,128)(2,1)S(1)}, bf16[192,768]{1,0:T(8,128)(2,1)}, u32[]{:S(2)}, u32[]{:S(2)}) collective-permute-start(bf16[192,768]{1,0:T(8,128)(2,1)S(1)} %bitcast.59), channel_id=1, source_target_pairs={{0,12},{4,8},{8,4},{12,0},{1,13},{5,9},{9,5},{13,1},{2,14},{6,10},... | collective-permute-start | bytes 884744 | tf_op jit(solution)/shard_map/ppermute | solution.py:47
  42.9 42.4 %collective-permute-start.20 = (bf16[192,768]{1,0:T(8,128)(2,1)S(1)}, bf16[192,768]{1,0:T(8,128)(2,1)S(1)}, u32[]{:S(2)}, u32[]{:S(2)}) collective-permute-start(bf16[192,768]{1,0:T(8,128)(2,1)S(1)} %bitcast.60), channel_id=1, source_target_pairs={{0,8},{4,12},{8,0},{12,4},{1,9},{5,13},{9,1},{13,5},{2,10},{6,14},... | collective-permute-start | bytes 884744 | tf_op jit(solution)/shard_map/ppermute | solution.py:47
  43.6 30.6 %collective-permute-start.19 = (bf16[192,768]{1,0:T(8,128)(2,1)S(1)}, bf16[192,768]{1,0:T(8,128)(2,1)S(1)}, u32[]{:S(2)}, u32[]{:S(2)}) collective-permute-start(bf16[192,768]{1,0:T(8,128)(2,1)S(1)} %bitcast.61), channel_id=1, source_target_pairs={{0,4},{4,0},{8,12},{12,8},{1,5},{5,1},{9,13},{13,9},{2,6},{6,2},{1... | collective-permute-start | bytes 884744 | tf_op jit(solution)/shard_map/ppermute | solution.py:47
  63.6 26.4 %collective-permute-start.4 = (bf16[3,768,192]{1,2,0:T(8,128)(2,1)}, bf16[3,768,192]{1,2,0:T(8,128)(2,1)}, u32[]{:S(2)}, u32[]{:S(2)}) collective-permute-start(bf16[3,768,192]{1,2,0:T(8,128)(2,1)} %copy.27), channel_id=1, source_target_pairs={{0,16},{16,0},{1,17},{17,1},{2,18},{18,2},{3,19},{19,3},{4,20},{20... | collective-permute-start | bytes 2654216 | tf_op jit(solution)/shard_map/ppermute | solution.py:47
  66.3 21.3 %collective-permute-start.21 = (bf16[192,768]{1,0:T(8,128)(2,1)S(1)}, bf16[192,768]{1,0:T(8,128)(2,1)S(1)}, u32[]{:S(2)}, u32[]{:S(2)}) collective-permute-start(bf16[192,768]{1,0:T(8,128)(2,1)S(1)} %bitcast.62), channel_id=1, source_target_pairs={{0,12},{4,8},{8,4},{12,0},{1,13},{5,9},{9,5},{13,1},{2,14},{6,10},... | collective-permute-start | bytes 884744 | tf_op jit(solution)/shard_map/ppermute | solution.py:47
  70.0 24.8 %collective-permute-start.11 = (bf16[256,768]{1,0:T(8,128)(2,1)S(1)}, bf16[256,768]{1,0:T(8,128)(2,1)S(1)}, u32[]{:S(2)}, u32[]{:S(2)}) collective-permute-start(bf16[256,768]{1,0:T(8,128)(2,1)S(1)} %norm_first.1.refs_4_.refs_5_), channel_id=1, source_target_pairs={{0,3},{1,2},{2,1},{3,0},{4,7},{5,6},{6,5},{7,4},{8,11},{9,10},{10,... | collective-permute-start | bytes 1179656 | tf_op jit(solution)/shard_map/ppermute | solution.py:47
  89.9 42.6 %collective-permute-start.22 = (bf16[768,768]{1,0:T(8,128)(2,1)}, bf16[768,768]{1,0:T(8,128)(2,1)}, u32[]{:S(2)}, u32[]{:S(2)}) collective-permute-start(bf16[768,768]{1,0:T(8,128)(2,1)} %constant_dynamic-update-slice_fusion), channel_id=1, source_target_pairs={{0,16},{16,0},{1,17},{17,1},{2,18},{18,2},{3,19},{19,3},{4,20},{20... | collective-permute-start | bytes 3538952 | tf_op jit(solution)/shard_map/ppermute | solution.py:47
  90.0 45.4 %collective-permute-start.18 = (bf16[768,768]{1,0:T(8,128)(2,1)}, bf16[768,768]{1,0:T(8,128)(2,1)}, u32[]{:S(2)}, u32[]{:S(2)}) collective-permute-start(bf16[768,768]{1,0:T(8,128)(2,1)} %constant_dynamic-update-slice_fusion.4), channel_id=1, source_target_pairs={{0,16},{16,0},{1,17},{17,1},{2,18},{18,2},{3,19},{19,3},{4,20},{20... | collective-permute-start | bytes 3538952 | tf_op jit(solution)/shard_map/ppermute | solution.py:47
  153.0 19.2 %collective-permute-start.27 = (bf16[256,768]{1,0:T(8,128)(2,1)S(1)}, bf16[256,768]{1,0:T(8,128)(2,1)S(1)}, u32[]{:S(2)}, u32[]{:S(2)}) collective-permute-start(bf16[256,768]{1,0:T(8,128)(2,1)S(1)} %get-tuple-element.102), channel_id=1, source_target_pairs={{0,2},{1,3},{2,0},{3,1},{4,6},{5,7},{6,4},{7,5},{8,10},{9,11},{10,... | collective-permute-start | bytes 1179656 | tf_op jit(solution)/shard_map/ppermute | solution.py:47
  153.8 18.4 %collective-permute-start.28 = (bf16[256,768]{1,0:T(8,128)(2,1)S(1)}, bf16[256,768]{1,0:T(8,128)(2,1)S(1)}, u32[]{:S(2)}, u32[]{:S(2)}) collective-permute-start(bf16[256,768]{1,0:T(8,128)(2,1)S(1)} %get-tuple-element.103), channel_id=1, source_target_pairs={{0,3},{1,2},{2,1},{3,0},{4,7},{5,6},{6,5},{7,4},{8,11},{9,10},{10,... | collective-permute-start | bytes 1179656 | tf_op jit(solution)/shard_map/ppermute | solution.py:47
  224.1 24.9 %collective-permute-start.36 = (bf16[256,768]{1,0:T(8,128)(2,1)}, bf16[256,768]{1,0:T(8,128)(2,1)}, u32[]{:S(2)}, u32[]{:S(2)}) collective-permute-start(bf16[256,768]{1,0:T(8,128)(2,1)} %get-tuple-element.111.refs_3_.refs_2_), channel_id=1, source_target_pairs={{0,2},{1,3},{2,0},{3,1},{4,6},{5,7},{6,4},{7,5},{8,10},{9,11},{10,... | collective-permute-start | bytes 1179656 | tf_op jit(solution)/shard_map/ppermute | solution.py:47
  225.4 23.6 %collective-permute-start.35 = (bf16[256,768]{1,0:T(8,128)(2,1)}, bf16[256,768]{1,0:T(8,128)(2,1)}, u32[]{:S(2)}, u32[]{:S(2)}) collective-permute-start(bf16[256,768]{1,0:T(8,128)(2,1)} %get-tuple-element.111.refs_3_.refs_2_), channel_id=1, source_target_pairs={{0,1},{1,0},{2,3},{3,2},{4,5},{5,4},{6,7},{7,6},{8,9},{9,8},{10,11... | collective-permute-start | bytes 1179656 | tf_op jit(solution)/shard_map/ppermute | solution.py:47
  228.2 27.9 %collective-permute-start.44 = (bf16[256,768]{1,0:T(8,128)(2,1)S(1)}, bf16[256,768]{1,0:T(8,128)(2,1)S(1)}, u32[]{:S(2)}, u32[]{:S(2)}) collective-permute-start(bf16[256,768]{1,0:T(8,128)(2,1)S(1)} %bitcast_select_fusion.refs_3_.refs_0_.refs_6_), channel_id=1, source_target_pairs={{0,3},{1,2},{2,1},{3,0},{4,7},{5,6},{6,5},{7,4},{8,11},{9,10},{10,... | collective-permute-start | bytes 1179656 | tf_op jit(solution)/shard_map/ppermute | solution.py:47
  230.0 28.1 %collective-permute-start.43 = (bf16[256,768]{1,0:T(8,128)(2,1)S(1)}, bf16[256,768]{1,0:T(8,128)(2,1)S(1)}, u32[]{:S(2)}, u32[]{:S(2)}) collective-permute-start(bf16[256,768]{1,0:T(8,128)(2,1)S(1)} %bitcast_select_fusion.refs_3_.refs_0_.refs_6_), channel_id=1, source_target_pairs={{0,2},{1,3},{2,0},{3,1},{4,6},{5,7},{6,4},{7,5},{8,10},{9,11},{10,... | collective-permute-start | bytes 1179656 | tf_op jit(solution)/shard_map/ppermute | solution.py:47
  235.6 23.2 %collective-permute-start.42 = (bf16[256,768]{1,0:T(8,128)(2,1)S(1)}, bf16[256,768]{1,0:T(8,128)(2,1)S(1)}, u32[]{:S(2)}, u32[]{:S(2)}) collective-permute-start(bf16[256,768]{1,0:T(8,128)(2,1)S(1)} %bitcast_select_fusion.refs_3_.refs_0_.refs_6_), channel_id=1, source_target_pairs={{0,1},{1,0},{2,3},{3,2},{4,5},{5,4},{6,7},{7,6},{8,9},{9,8},{10,11... | collective-permute-start | bytes 1179656 | tf_op jit(solution)/shard_map/ppermute | solution.py:47
  262.1 20.4 %collective-permute-start.46 = (bf16[256,768]{1,0:T(8,128)(2,1)S(1)}, bf16[256,768]{1,0:T(8,128)(2,1)S(1)}, u32[]{:S(2)}, u32[]{:S(2)}) collective-permute-start(bf16[256,768]{1,0:T(8,128)(2,1)S(1)} %get-tuple-element.119), channel_id=1, source_target_pairs={{0,2},{1,3},{2,0},{3,1},{4,6},{5,7},{6,4},{7,5},{8,10},{9,11},{10,... | collective-permute-start | bytes 1179656 | tf_op jit(solution)/shard_map/ppermute | solution.py:47
  262.8 19.8 %collective-permute-start.47 = (bf16[256,768]{1,0:T(8,128)(2,1)S(1)}, bf16[256,768]{1,0:T(8,128)(2,1)S(1)}, u32[]{:S(2)}, u32[]{:S(2)}) collective-permute-start(bf16[256,768]{1,0:T(8,128)(2,1)S(1)} %get-tuple-element.120), channel_id=1, source_target_pairs={{0,3},{1,2},{2,1},{3,0},{4,7},{5,6},{6,5},{7,4},{8,11},{9,10},{10,... | collective-permute-start | bytes 1179656 | tf_op jit(solution)/shard_map/ppermute | solution.py:47
  265.3 25.5 %collective-permute-start.38 = (bf16[256,768]{1,0:T(8,128)(2,1)S(1)}, bf16[256,768]{1,0:T(8,128)(2,1)S(1)}, u32[]{:S(2)}, u32[]{:S(2)}) collective-permute-start(bf16[256,768]{1,0:T(8,128)(2,1)S(1)} %get-tuple-element.113), channel_id=1, source_target_pairs={{0,1},{1,0},{2,3},{3,2},{4,5},{5,4},{6,7},{7,6},{8,9},{9,8},{10,11... | collective-permute-start | bytes 1179656 | tf_op jit(solution)/shard_map/ppermute | solution.py:47
  265.5 42.1 %collective-permute-start.39 = (bf16[256,768]{1,0:T(8,128)(2,1)S(1)}, bf16[256,768]{1,0:T(8,128)(2,1)S(1)}, u32[]{:S(2)}, u32[]{:S(2)}) collective-permute-start(bf16[256,768]{1,0:T(8,128)(2,1)S(1)} %get-tuple-element.114), channel_id=1, source_target_pairs={{0,2},{1,3},{2,0},{3,1},{4,6},{5,7},{6,4},{7,5},{8,10},{9,11},{10,... | collective-permute-start | bytes 1179656 | tf_op jit(solution)/shard_map/ppermute | solution.py:47
  273.9 36.1 %collective-permute-start.40 = (bf16[256,768]{1,0:T(8,128)(2,1)S(1)}, bf16[256,768]{1,0:T(8,128)(2,1)S(1)}, u32[]{:S(2)}, u32[]{:S(2)}) collective-permute-start(bf16[256,768]{1,0:T(8,128)(2,1)S(1)} %get-tuple-element.115), channel_id=1, source_target_pairs={{0,3},{1,2},{2,1},{3,0},{4,7},{5,6},{6,5},{7,4},{8,11},{9,10},{10,... | collective-permute-start | bytes 1179656 | tf_op jit(solution)/shard_map/ppermute | solution.py:47
  284.2 26.2 %collective-permute-start.50 = (bf16[256,768]{1,0:T(8,128)(2,1)S(1)}, bf16[256,768]{1,0:T(8,128)(2,1)S(1)}, u32[]{:S(2)}, u32[]{:S(2)}) collective-permute-start(bf16[256,768]{1,0:T(8,128)(2,1)S(1)} %get-tuple-element.126.refs_7_.refs_9_), channel_id=1, source_target_pairs={{0,3},{1,2},{2,1},{3,0},{4,7},{5,6},{6,5},{7,4},{8,11},{9,10},{10,... | collective-permute-start | bytes 1179656 | tf_op jit(solution)/shard_map/ppermute | solution.py:47
  286.2 28.7 %collective-permute-start.49 = (bf16[256,768]{1,0:T(8,128)(2,1)S(1)}, bf16[256,768]{1,0:T(8,128)(2,1)S(1)}, u32[]{:S(2)}, u32[]{:S(2)}) collective-permute-start(bf16[256,768]{1,0:T(8,128)(2,1)S(1)} %get-tuple-element.126.refs_7_.refs_9_), channel_id=1, source_target_pairs={{0,2},{1,3},{2,0},{3,1},{4,6},{5,7},{6,4},{7,5},{8,10},{9,11},{10,... | collective-permute-start | bytes 1179656 | tf_op jit(solution)/shard_map/ppermute | solution.py:47
  290.8 24.1 %collective-permute-start.48 = (bf16[256,768]{1,0:T(8,128)(2,1)S(1)}, bf16[256,768]{1,0:T(8,128)(2,1)S(1)}, u32[]{:S(2)}, u32[]{:S(2)}) collective-permute-start(bf16[256,768]{1,0:T(8,128)(2,1)S(1)} %get-tuple-element.126.refs_7_.refs_9_), channel_id=1, source_target_pairs={{0,1},{1,0},{2,3},{3,2},{4,5},{5,4},{6,7},{7,6},{8,9},{9,8},{10,11... | collective-permute-start | bytes 1179656 | tf_op jit(solution)/shard_map/ppermute | solution.py:47
  307.7 52.2 %collective-permute-start.97 = (bf16[768,768]{1,0:T(8,128)(2,1)}, bf16[768,768]{1,0:T(8,128)(2,1)}, u32[]{:S(2)}, u32[]{:S(2)}) collective-permute-start(bf16[768,768]{1,0:T(8,128)(2,1)} %get-tuple-element.173), channel_id=1, source_target_pairs={{0,16},{1,17},{2,18},{3,19},{4,20},{5,21},{6,22},{7,23},{8,24},{9,... | collective-permute-start | bytes 3538952 | tf_op jit(solution)/shard_map/ppermute | solution.py:309
  310.3 26.3 %collective-permute-start.41 = (bf16[256,768]{1,0:T(8,128)(2,1)S(1)}, bf16[256,768]{1,0:T(8,128)(2,1)S(1)}, u32[]{:S(2)}, u32[]{:S(2)}) collective-permute-start(bf16[256,768]{1,0:T(8,128)(2,1)S(1)} %broadcast_select_fusion.10), channel_id=1, source_target_pairs={{0,16},{16,0},{1,17},{17,1},{2,18},{18,2},{3,19},{19,3},{4,20},{20... | collective-permute-start | bytes 1179656 | tf_op jit(solution)/shard_map/ppermute | solution.py:47
  341.6 38.9 %collective-permute-start.105 = (bf16[768,768]{1,0:T(8,128)(2,1)}, bf16[768,768]{1,0:T(8,128)(2,1)S(1)}, u32[]{:S(2)}, u32[]{:S(2)}) collective-permute-start(bf16[768,768]{1,0:T(8,128)(2,1)} %copy-done.10), channel_id=1, source_target_pairs={{0,16},{1,17},{2,18},{3,19},{4,20},{5,21},{6,22},{7,23},{8,24},{9,... | collective-permute-start | bytes 3538952 | tf_op jit(solution)/shard_map/ppermute | solution.py:309
  359.9 46.7 %collective-permute-start.81 = (bf16[3,768,192]{1,2,0:T(8,128)(2,1)S(1)}, bf16[3,768,192]{1,2,0:T(8,128)(2,1)S(1)}, u32[]{:S(2)}, u32[]{:S(2)}) collective-permute-start(bf16[3,768,192]{1,2,0:T(8,128)(2,1)S(1)} %copy-done.108), channel_id=1, source_target_pairs={{0,16},{1,17},{2,18},{3,19},{4,20},{5,21},{6,22},{7,23},{8,24},{9,... | collective-permute-start | bytes 2654216 | tf_op jit(solution)/shard_map/ppermute | solution.py:309
  376.8 18.9 %collective-permute-start.58 = (bf16[256,768]{1,0:T(8,128)(2,1)S(1)}, bf16[256,768]{1,0:T(8,128)(2,1)S(1)}, u32[]{:S(2)}, u32[]{:S(2)}) collective-permute-start(bf16[256,768]{1,0:T(8,128)(2,1)S(1)} %get-tuple-element.135), channel_id=1, source_target_pairs={{0,2},{1,3},{2,0},{3,1},{4,6},{5,7},{6,4},{7,5},{8,10},{9,11},{10,... | collective-permute-start | bytes 1179656 | tf_op jit(solution)/shard_map/ppermute | solution.py:47
  380.4 68.5 %collective-permute-start.90 = (bf16[192,192]{1,0:T(8,128)(2,1)}, bf16[192,192]{1,0:T(8,128)(2,1)}, u32[]{:S(2)}, u32[]{:S(2)}) collective-permute-start(bf16[192,192]{1,0:T(8,128)(2,1)} %get-tuple-element.233), channel_id=1, source_target_pairs={{16,20},{20,16},{24,28},{28,24},{17,21},{21,17},{25,29},{29,25},{1... | collective-permute-start | bytes 221192 | tf_op jit(solution)/shard_map/ppermute | solution.py:319
  407.5 53.2 %collective-permute-start.92 = (bf16[192,192]{1,0:T(8,128)(2,1)}, bf16[192,192]{1,0:T(8,128)(2,1)}, u32[]{:S(2)}, u32[]{:S(2)}) collective-permute-start(bf16[192,192]{1,0:T(8,128)(2,1)} %get-tuple-element.234), channel_id=1, source_target_pairs={{16,28},{20,24},{24,20},{28,16},{17,29},{21,25},{25,21},{29,17},{1... | collective-permute-start | bytes 221192 | tf_op jit(solution)/shard_map/ppermute | solution.py:319
  411.2 66.7 %collective-permute-start.93 = (bf16[768,768]{1,0:T(8,128)(2,1)}, bf16[768,768]{1,0:T(8,128)(2,1)}, u32[]{:S(2)}, u32[]{:S(2)}) collective-permute-start(bf16[768,768]{1,0:T(8,128)(2,1)} %copy-done.16), channel_id=1, source_target_pairs={{16,0},{17,1},{18,2},{19,3},{20,4},{21,5},{22,6},{23,7},{24,8},{25... | collective-permute-start | bytes 3538952 | tf_op jit(solution)/shard_map/ppermute | solution.py:309
  416.5 64.7 %collective-permute-start.101 = (bf16[768,768]{1,0:T(8,128)(2,1)}, bf16[768,768]{1,0:T(8,128)(2,1)}, u32[]{:S(2)}, u32[]{:S(2)}) collective-permute-start(bf16[768,768]{1,0:T(8,128)(2,1)} %copy-done.14), channel_id=1, source_target_pairs={{16,0},{17,1},{18,2},{19,3},{20,4},{21,5},{22,6},{23,7},{24,8},{25... | collective-permute-start | bytes 3538952 | tf_op jit(solution)/shard_map/ppermute | solution.py:309
  447.1 19.0 %collective-permute-start.91 = (bf16[192,192]{1,0:T(8,128)(2,1)}, bf16[192,192]{1,0:T(8,128)(2,1)S(1)}, u32[]{:S(2)}, u32[]{:S(2)}) collective-permute-start(bf16[192,192]{1,0:T(8,128)(2,1)} %get-tuple-element.235), channel_id=1, source_target_pairs={{16,24},{20,28},{24,16},{28,20},{17,25},{21,29},{25,17},{29,21},{1... | collective-permute-start | bytes 221192 | tf_op jit(solution)/shard_map/ppermute | solution.py:319
  448.9 19.8 %collective-permute-start.86 = (bf16[192,192]{1,0:T(8,128)(2,1)S(1)}, bf16[192,192]{1,0:T(8,128)(2,1)S(1)}, u32[]{:S(2)}, u32[]{:S(2)}) collective-permute-start(bf16[192,192]{1,0:T(8,128)(2,1)S(1)} %get-tuple-element.230), channel_id=1, source_target_pairs={{0,4},{4,0},{8,12},{12,8},{1,5},{5,1},{9,13},{13,9},{2,6},{6,2},{1... | collective-permute-start | bytes 221192 | tf_op jit(solution)/shard_map/ppermute | solution.py:319
  468.7 46.9 %collective-permute-start.98 = (bf16[192,768]{1,0:T(8,128)(2,1)}, bf16[192,768]{1,0:T(8,128)(2,1)}, u32[]{:S(2)}, u32[]{:S(2)}) collective-permute-start(bf16[192,768]{1,0:T(8,128)(2,1)} %get-tuple-element.215), channel_id=1, source_target_pairs={{16,20},{20,16},{24,28},{28,24},{17,21},{21,17},{25,29},{29,25},{1... | collective-permute-start | bytes 884744 | tf_op jit(solution)/shard_map/ppermute | solution.py:319
  481.2 37.2 %collective-permute-start.100 = (bf16[192,768]{1,0:T(8,128)(2,1)S(1)}, bf16[192,768]{1,0:T(8,128)(2,1)S(1)}, u32[]{:S(2)}, u32[]{:S(2)}) collective-permute-start(bf16[192,768]{1,0:T(8,128)(2,1)S(1)} %copy-done.111), channel_id=1, source_target_pairs={{16,28},{20,24},{24,20},{28,16},{17,29},{21,25},{25,21},{29,17},{1... | collective-permute-start | bytes 884744 | tf_op jit(solution)/shard_map/ppermute | solution.py:319
  521.7 27.3 %collective-permute-start.95 = (bf16[192,768]{1,0:T(8,128)(2,1)S(1)}, bf16[192,768]{1,0:T(8,128)(2,1)S(1)}, u32[]{:S(2)}, u32[]{:S(2)}) collective-permute-start(bf16[192,768]{1,0:T(8,128)(2,1)S(1)} %get-tuple-element.214), channel_id=1, source_target_pairs={{0,8},{4,12},{8,0},{12,4},{1,9},{5,13},{9,1},{13,5},{2,10},{6,14},... | collective-permute-start | bytes 884744 | tf_op jit(solution)/shard_map/ppermute | solution.py:319
  524.9 37.1 %collective-permute-start.77 = (bf16[3,768,192]{1,2,0:T(8,128)(2,1)}, bf16[3,768,192]{1,2,0:T(8,128)(2,1)}, u32[]{:S(2)}, u32[]{:S(2)}) collective-permute-start(bf16[3,768,192]{1,2,0:T(8,128)(2,1)} %copy.31), channel_id=1, source_target_pairs={{16,0},{17,1},{18,2},{19,3},{20,4},{21,5},{22,6},{23,7},{24,8},{25... | collective-permute-start | bytes 2654216 | tf_op jit(solution)/shard_map/ppermute | solution.py:309
  526.8 28.2 %collective-permute-start.107 = (bf16[192,768]{1,0:T(8,128)(2,1)}, bf16[192,768]{1,0:T(8,128)(2,1)}, u32[]{:S(2)}, u32[]{:S(2)}) collective-permute-start(bf16[192,768]{1,0:T(8,128)(2,1)} %get-tuple-element.211), channel_id=1, source_target_pairs={{16,24},{20,28},{24,16},{28,20},{17,25},{21,29},{25,17},{29,21},{1... | collective-permute-start | bytes 884744 | tf_op jit(solution)/shard_map/ppermute | solution.py:319
  528.2 28.2 %collective-permute-start.102 = (bf16[192,768]{1,0:T(8,128)(2,1)}, bf16[192,768]{1,0:T(8,128)(2,1)}, u32[]{:S(2)}, u32[]{:S(2)}) collective-permute-start(bf16[192,768]{1,0:T(8,128)(2,1)} %get-tuple-element.206), channel_id=1, source_target_pairs={{0,4},{4,0},{8,12},{12,8},{1,5},{5,1},{9,13},{13,9},{2,6},{6,2},{1... | collective-permute-start | bytes 884744 | tf_op jit(solution)/shard_map/ppermute | solution.py:319
  531.9 25.8 %collective-permute-start.104 = (bf16[192,768]{1,0:T(8,128)(2,1)}, bf16[192,768]{1,0:T(8,128)(2,1)}, u32[]{:S(2)}, u32[]{:S(2)}) collective-permute-start(bf16[192,768]{1,0:T(8,128)(2,1)} %get-tuple-element.207), channel_id=1, source_target_pairs={{0,12},{4,8},{8,4},{12,0},{1,13},{5,9},{9,5},{13,1},{2,14},{6,10},... | collective-permute-start | bytes 884744 | tf_op jit(solution)/shard_map/ppermute | solution.py:319
  556.4 19.3 %collective-permute-start.84 = (bf16[3,192,192]{2,1,0:T(8,128)(2,1)}, bf16[3,192,192]{2,1,0:T(8,128)(2,1)}, u32[]{:S(2)}, u32[]{:S(2)}) collective-permute-start(bf16[3,192,192]{2,1,0:T(8,128)(2,1)} %get-tuple-element.222), channel_id=1, source_target_pairs={{16,28},{20,24},{24,20},{28,16},{17,29},{21,25},{25,21},{29,17},{1... | collective-permute-start | bytes 663560 | tf_op jit(solution)/shard_map/ppermute | solution.py:319
  (191 other events, 2912.3 us)
